TPU v7x, 32 devices: a whole 2x2x4 slice. The times are simulated.
32 devices in a mesh: dp: 16 (over z, y, x), tensor: 2 (over core).
Axes of the slice: x: 2, y: 2, z: 4, core: 2. Of those that a mesh axis runs over, the one named last changes fastest.
Arguments:
- grad_kv: bfloat16 [16, 2, 512, 2048], P('dp', None, 'tensor'), may hold values from -6 to 6
- error_kv: bfloat16 [16, 2, 512, 2048], P('dp', None, 'tensor'), may hold values from -4 to 4
- moment_kv: bfloat16 [16, 2, 512, 2048], P('dp', None, 'tensor'), may hold values from -6 to 6
- start_dirs: float32 [2, 32, 2048], replicated, may hold values from -6 to 6
- weight_kv: float32 [2, 512, 2048], P(None, 'tensor', 'dp'), may hold values from -6 to 6
- norm_grads: bfloat16 [16, 2, 2048], P('dp', None, 'tensor'), may hold values from -6 to 6
- norm_gains: float32 [2, 2, 1024], P(None, 'tensor', 'dp'), may hold values from 0.5 to 1.5
Outputs:
- new_weight_kv: float32 [2, 512, 2048], P(None, 'tensor', 'dp')
- new_error_kv: bfloat16 [16, 2, 512, 2048], P('dp', None, 'tensor')
- new_moment_kv: bfloat16 [16, 2, 512, 2048], P('dp', None, 'tensor')
- new_gains: float32 [2, 2, 1024], P(None, 'tensor', 'dp')
All inputs are finite; a program needn't handle non-finite values.
Results may differ from a plain program's by a relative error of at most 0.001.
Values sent between devices are 32-bit elements; how exact they have to be, the bound alone decides.
A program may use at most 64 MiB of HBM per device.

v0:
```python
import jax
import jax.numpy as jnp
from jax import lax
from jax.sharding import PartitionSpec as P

momentum_decay = 0.9
step_size = 0.5


def project(inputs, directions):
    return jnp.einsum("mrd,mkd->mrk", inputs, directions, precision=lax.Precision.HIGHEST)


def tri_solve(triangle, columns):
    return jax.scipy.linalg.solve_triangular(triangle, columns, lower=True)


def orthonormal(factor):
    full_rows = lax.all_gather(factor, "tensor", axis=1, tiled=True)
    gram_matrix = jnp.einsum("mrk,mrj->mkj", full_rows, full_rows, precision=lax.Precision.HIGHEST)
    cholesky_factor = jnp.linalg.cholesky(gram_matrix)
    solved = jax.vmap(tri_solve)(cholesky_factor, jnp.swapaxes(factor, 1, 2))
    return jnp.swapaxes(solved, 1, 2)


def column_sums(inputs, basis):
    partial_sum = jnp.einsum("mrd,mrk->mkd", inputs, basis, precision=lax.Precision.HIGHEST)
    summed = lax.psum(partial_sum, ("dp", "tensor"))
    return summed


def shards(grad_kv, error_kv, moment_kv, start_dirs, weight_kv, norm_grads, norm_gains):
    replicas = lax.axis_size("dp")
    dp_index = lax.axis_index("dp")
    moment_f = momentum_decay * moment_kv.astype(jnp.float32) + grad_kv.astype(jnp.float32)
    new_moment_kv = moment_f.astype(jnp.bfloat16)
    inputs = (moment_f + error_kv.astype(jnp.float32))[0]
    norm_terms = norm_grads[0].astype(jnp.float32)
    gain_cols = norm_gains.shape[2]
    factor = project(inputs, start_dirs)
    factor, norm_total = lax.psum((factor, norm_terms), "dp")
    own_norm = lax.dynamic_slice_in_dim(norm_total, dp_index * gain_cols, gain_cols, 1)
    mean_norm = own_norm / replicas
    basis = orthonormal(factor)
    directions = column_sums(inputs, basis)
    factor = lax.psum(project(inputs, directions), "dp")
    basis = orthonormal(factor)
    directions = column_sums(inputs, basis)
    approx = (
        jnp.einsum("mrk,mkd->mrd", basis, directions, precision=lax.Precision.HIGHEST) / replicas
    )
    new_error_kv = (inputs - approx).astype(jnp.bfloat16)[None]
    weight_cols = weight_kv.shape[2]
    own_approx = lax.dynamic_slice_in_dim(approx, dp_index * weight_cols, weight_cols, 2)
    new_weight_kv = weight_kv - step_size * own_approx
    new_gains = norm_gains - step_size * mean_norm[:, None, :]
    return (new_weight_kv, new_error_kv, new_moment_kv, new_gains)


def solution(mesh):
    return jax.shard_map(
        shards,
        mesh=mesh,
        in_specs=(
            P("dp", None, "tensor", None),
            P("dp", None, "tensor", None),
            P("dp", None, "tensor", None),
            P(),
            P(None, "tensor", "dp"),
            P("dp", None, "tensor"),
            P(None, "tensor", "dp"),
        ),
        out_specs=(
            P(None, "tensor", "dp"),
            P("dp", None, "tensor", None),
            P("dp", None, "tensor", None),
            P(None, "tensor", "dp"),
        ),
        check_vma=False,
    )
```

profile of v0, /device:TPU:0, one launch (start us, length us, event | category | flops | bytes accessed | tf_op | source)
XLA Modules:
  0.0 541.1 jit_solution(2361031230973301749)
XLA Ops:
  7.2 1.0 copy-done
  8.2 8.1 %fusion.6 = f32[2,256,32]{1,2,0:T(8,128)} fusion(f32[2,32,2048]{2,1,0:T(8,128)S(1)} %copy-done, bf16[1,2,256,2048]{3,2,1,0:T(8,128)(2,1)} %param.11, bf16[1,2,256,2048]{3,2,1,0:T(8,128)(2,1)} %param.10, bf16[1,2,256,2048]{3,2,1,0:T(8,128)(2,1)} %param.12), kind=kOutput, calls=%fused_computation.7 | convolution fusion | flops 408944640 | bytes 6881280 | tf_op jit(solution)/shard_map/mrd,mkd->mrk/dot_general | solution.py:11
  16.4 104.7 %all-reduce.5.cloned.1.call-done = f32[2,256,32]{1,2,0:T(8,128)} async-done(((f32[2,256,32]{1,2,0:T(8,128)}), f32[2,256,32]{1,2,0:T(8,128)}) %all-reduce.5.cloned.1.call-update) | async-done | bytes 65552 | tf_op jit(solution)/shard_map/psum | solution.py:41
  121.2 2.3 all_gather.6
  123.5 0.2 fusion.19
  123.7 0.1 copy.16
  123.8 5.9 %custom-call.8 = f32[2,32,32]{2,1,0:T(8,128)S(1)} custom-call(f32[2,32,32]{2,1,0:T(8,128)S(1)} %fusion.18), custom_call_target="Cholesky" | custom-call | tf_op jit(solution)/shard_map/jit(cholesky)/cholesky | solution.py:21
  129.7 0.1 compare_reduce_fusion.1
  129.8 0.1 select_bitcast_fusion.1
  129.9 4.9 custom-call.9
  134.8 1.1 fusion.13
  136.0 6.2 %fusion.4 = f32[2,32,2048]{2,1,0:T(8,128)} fusion(f32[2,32,256]{2,1,0:T(8,128)S(1)} %fusion.13, bf16[1,2,256,2048]{3,2,1,0:T(8,128)(2,1)} %param.11, bf16[1,2,256,2048]{3,2,1,0:T(8,128)(2,1)S(1)} %copy-done.1, bf16[1,2,256,2048]{3,2,1,0:T(8,128)(2,1)} %param.12), kind=kOutput, calls=%fused_computation.5 | convolution fusion | flops 408944640 | bytes 6881280 | tf_op jit(solution)/shard_map/mrd,mrk->mkd/dot_general | solution.py:27
  142.2 127.0 %all-reduce.7.cloned.1.call-done = f32[2,32,2048]{2,1,0:T(8,128)} async-done(((f32[2,32,2048]{2,1,0:T(8,128)}), f32[2,32,2048]{2,1,0:T(8,128)}) %all-reduce.7.cloned.1.call-update) | async-done | bytes 524304 | tf_op jit(solution)/shard_map/psum | solution.py:28
  269.2 7.6 %fusion.2 = f32[2,256,32]{1,2,0:T(8,128)} fusion(f32[2,32,2048]{2,1,0:T(8,128)} %all-reduce.7.cloned.1.call-done, bf16[1,2,256,2048]{3,2,1,0:T(8,128)(2,1)} %param.11, bf16[1,2,256,2048]{3,2,1,0:T(8,128)(2,1)S(1)} %copy-done.1, bf16[1,2,256,2048]{3,2,1,0:T(8,128)(2,1)} %param.12), kind=kOutput, calls=%fused_computation.3 | convolution fusion | flops 408944640 | bytes 6881280 | tf_op jit(solution)/shard_map/mrd,mkd->mrk/dot_general | solution.py:11
  276.8 0.2 all-reduce.11.cloned.1.call-start
  277.1 3.9 fusion.9
  281.0 97.0 %all-reduce.9.cloned.1.call-done = f32[2,256,32]{1,2,0:T(8,128)} async-done(((f32[2,256,32]{1,2,0:T(8,128)}), f32[2,256,32]{1,2,0:T(8,128)}) %all-reduce.9.cloned.1.call-update) | async-done | bytes 65552 | tf_op jit(solution)/shard_map/psum | solution.py:46
  378.0 2.3 all_gather.7
  380.2 0.2 fusion.20
  380.5 0.1 copy.17
  380.6 5.9 %custom-call.10 = f32[2,32,32]{2,1,0:T(8,128)S(1)} custom-call(f32[2,32,32]{2,1,0:T(8,128)S(1)} %fusion.16), custom_call_target="Cholesky" | custom-call | tf_op jit(solution)/shard_map/jit(cholesky)/cholesky | solution.py:21
  386.5 0.1 compare_reduce_fusion
  386.6 0.1 select_bitcast_fusion
  386.7 4.9 custom-call.11
  391.6 1.1 fusion.11
  392.7 6.2 %fusion = f32[2,32,2048]{2,1,0:T(8,128)} fusion(f32[2,32,256]{2,1,0:T(8,128)S(1)} %fusion.11, bf16[1,2,256,2048]{3,2,1,0:T(8,128)(2,1)} %param.11, bf16[1,2,256,2048]{3,2,1,0:T(8,128)(2,1)S(1)} %copy-done.1, bf16[1,2,256,2048]{3,2,1,0:T(8,128)(2,1)} %param.12), kind=kOutput, calls=%fused_computation.1 | convolution fusion | flops 408944640 | bytes 6881280 | tf_op jit(solution)/shard_map/mrd,mrk->mkd/dot_general | solution.py:27
  399.0 40.5 %psum.39 = f32[2,1024]{1,0:T(2,128)S(1)} all-reduce(f32[2,1024]{1,0:T(2,128)S(1)} %bitcast_convert_fusion), channel_id=1, replica_groups=mesh['dp'=16,'tensor'=2] {'dp'}, use_global_device_ids=true, to_apply=%region_6.9 | all-reduce | flops 2048 | bytes 16384 | tf_op jit(solution)/shard_map/psum | solution.py:41
  439.5 0.6 bitcast_subtract_fusion.1
  440.1 85.9 %all-reduce.11.cloned.1.call-done = f32[2,32,2048]{2,1,0:T(8,128)} async-done(((f32[2,32,2048]{2,1,0:T(8,128)}), f32[2,32,2048]{2,1,0:T(8,128)}) %all-reduce.11.cloned.1.call-update) | async-done | bytes 524304 | tf_op jit(solution)/shard_map/psum | solution.py:28
  526.0 4.7 convolution_multiply_fusion
  530.7 3.0 fusion.10
  533.8 0.7 multiply_subtract_fusion
  (27 shorter events, 0.3 us)
Async XLA Ops:
  7.2 1.0 copy-start
  7.2 128.8 %copy-start.1 = (bf16[1,2,256,2048]{3,2,1,0:T(8,128)(2,1)S(1)}, bf16[1,2,256,2048]{3,2,1,0:T(8,128)(2,1)}, u32[]{:S(2)}) copy-start(bf16[1,2,256,2048]{3,2,1,0:T(8,128)(2,1)} %param.10) | copy-start | bytes 6291460
  7.2 114.0 %all-reduce.5.cloned.1.call-start = ((), (), s32[]{:S(2)}) async-start(), calls=%async_computation | async-start | bytes 131072 | tf_op jit(solution)/shard_map/psum | solution.py:41
  16.4 252.9 %all-reduce.7.cloned.1.call-start = ((), (), s32[]{:S(2)}) async-start(), calls=%async_computation.1 | async-start | bytes 1048576 | tf_op jit(solution)/shard_map/psum | solution.py:28
  142.2 235.8 %all-reduce.9.cloned.1.call-start = ((), (), s32[]{:S(2)}) async-start(), calls=%async_computation.2 | async-start | bytes 131072 | tf_op jit(solution)/shard_map/psum | solution.py:46
  276.8 249.2 %all-reduce.11.cloned.1.call-start = ((), (), s32[]{:S(2)}) async-start(), calls=%async_computation.3 | async-start | bytes 1048576 | tf_op jit(solution)/shard_map/psum | solution.py:28
  281.0 118.0 %copy-start.5 = (bf16[1,2,1024]{2,1,0:T(2,128)(2,1)S(1)}, bf16[1,2,1024]{2,1,0:T(2,128)(2,1)}, u32[]{:S(2)}) copy-start(bf16[1,2,1024]{2,1,0:T(2,128)(2,1)} %param.15) | copy-start | bytes 12292
  281.0 158.5 %copy-start.6 = (f32[2,1,64]{2,1,0:T(1,128)S(1)}, f32[2,1,64]{2,1,0:T(1,128)}, u32[]{:S(2)}) copy-start(f32[2,1,64]{2,1,0:T(1,128)} %param.16) | copy-start | bytes 1540
  526.0 4.7 copy-start.2
  526.0 4.7 copy-start.3
  530.7 3.1 copy-start.4
Sparse Core Ops, SparseCore 0:
  16.5 104.6 all-reduce.4
  142.3 126.8 all-reduce.6
  277.0 100.9 all-reduce.8
  399.1 126.9 all-reduce.10
where the time goes:
time: 541 us
  waiting for transfers between devices  415 us (77%)
  blocking collectives  45 us (8%)
  matrix products  35.5 us (7%)
  other arithmetic  30.4 us (6%)
  between operations  13.9 us (3%)
    psum x2, waiting for transfers between devices, column_sums(): summed = lax.psum(partial_sum, ('dp', 'tensor'))  213 us
    psum x1, waiting for transfers between devices, shards(): factor, norm_total = lax.psum((factor, norm_terms), 'dp')  105 us
    psum x1, waiting for transfers between devices, shards(): factor = lax.psum(project(inputs, directions), 'dp')  97 us
    psum x1, blocking collectives, shards(): factor, norm_total = lax.psum((factor, norm_terms), 'dp')  40.5 us
    dot_general x2, matrix products, project(): jnp.einsum('mrd,mkd->mrk', inputs, directions, precision=lax.Precision.HI...  15.7 us
    dot_general x2, matrix products, column_sums(): jnp.einsum('mrd,mrk->mkd', inputs, basis, precision=lax.Precision.HIGHEST)  12.4 us
    another operation x7, other arithmetic, orthonormal(): cholesky_factor = jnp.linalg.cholesky(gram_matrix)  12 us
  transfers between devices with their start and end apart: 4, of which 4 were waited for; matrix products, arithmetic and copies ran while one was open for 1% of the time, Pallas kernels for 0%

commit v1 on v0

v1 whole, which is shorter than its diff:
```python
import functools

import jax
import jax.numpy as jnp
from jax import lax
from jax.experimental import pallas as pl
from jax.experimental.pallas import tpu as pltpu
from jax.sharding import PartitionSpec as P

momentum_decay = 0.9
step_size = 0.5
LANES = 128
SUBLANES = 8
F32 = jnp.float32
BF16 = jnp.bfloat16
HIGHEST = lax.Precision.HIGHEST


def project(inputs, directions):
    return jnp.einsum("mrd,mkd->mrk", inputs, directions, precision=HIGHEST)


def tri_solve(triangle, columns):
    return jax.scipy.linalg.solve_triangular(triangle, columns, lower=True)


def orthonormal(factor):
    full_rows = lax.all_gather(factor, "tensor", axis=1, tiled=True)
    gram_matrix = jnp.einsum("mrk,mrj->mkj", full_rows, full_rows, precision=HIGHEST)
    cholesky_factor = jnp.linalg.cholesky(gram_matrix)
    solved = jax.vmap(tri_solve)(cholesky_factor, jnp.swapaxes(factor, 1, 2))
    return jnp.swapaxes(solved, 1, 2)


def column_sums(inputs, basis):
    partial_sum = jnp.einsum("mrd,mrk->mkd", inputs, basis, precision=HIGHEST)
    return lax.psum(partial_sum, ("dp", "tensor"))


def plain_shards(grad_kv, error_kv, moment_kv, start_dirs, weight_kv, norm_grads, norm_gains):
    replicas = lax.axis_size("dp")
    dp_index = lax.axis_index("dp")
    moment_f = momentum_decay * moment_kv.astype(F32) + grad_kv.astype(F32)
    new_moment_kv = moment_f.astype(BF16)
    inputs = (moment_f + error_kv.astype(F32))[0]
    norm_terms = norm_grads[0].astype(F32)
    gain_cols = norm_gains.shape[2]
    factor = project(inputs, start_dirs)
    factor, norm_total = lax.psum((factor, norm_terms), "dp")
    own_norm = lax.dynamic_slice_in_dim(norm_total, dp_index * gain_cols, gain_cols, 1)
    mean_norm = own_norm / replicas
    basis = orthonormal(factor)
    directions = column_sums(inputs, basis)
    factor = lax.psum(project(inputs, directions), "dp")
    basis = orthonormal(factor)
    directions = column_sums(inputs, basis)
    approx = jnp.einsum("mrk,mkd->mrd", basis, directions, precision=HIGHEST) / replicas
    new_error_kv = (inputs - approx).astype(BF16)[None]
    weight_cols = weight_kv.shape[2]
    own_approx = lax.dynamic_slice_in_dim(approx, dp_index * weight_cols, weight_cols, 2)
    new_weight_kv = weight_kv - step_size * own_approx
    new_gains = norm_gains - step_size * mean_norm[:, None, :]
    return (new_weight_kv, new_error_kv, new_moment_kv, new_gains)


def split(value):
    high = value.astype(BF16)
    return high, (value - high.astype(F32)).astype(BF16)


def dot_nt(a, b):
    return lax.dot_general(a, b, (((1,), (1,)), ((), ())), preferred_element_type=F32)


def dot_tn(a, b):
    return lax.dot_general(a, b, (((0,), (0,)), ((), ())), preferred_element_type=F32)


def basis_of(factor, block=4):
    rank = factor.shape[0]
    gram = lax.dot_general(
        factor, factor, (((1,), (1,)), ((), ())), precision=HIGHEST, preferred_element_type=F32
    )
    row_id = lax.broadcasted_iota(jnp.int32, (rank, 2 * rank), 0)
    col_id = lax.broadcasted_iota(jnp.int32, (rank, 2 * rank), 1)
    unit = (lax.broadcasted_iota(jnp.int32, (rank, rank), 0) == lax.broadcasted_iota(jnp.int32, (rank, rank), 1)).astype(F32)
    work = jnp.concatenate([gram, unit], axis=1)
    for first in range(0, rank, block):
        cols = [jnp.broadcast_to(work[:, j : j + 1], work.shape) for j in range(first, first + block)]
        rows = [work[j : j + 1, :] for j in range(first, first + block)]
        for i in range(block):
            j = first + i
            ratio = jnp.where(row_id > j, cols[i] / cols[i][j : j + 1, :], 0.0)
            for k in range(i + 1, block):
                cols[k] = cols[k] - ratio * cols[k][j : j + 1, :]
                rows[k] = rows[k] - ratio[first + k : first + k + 1, :] * rows[i]
            work = work - ratio * rows[i]
    pivots = jnp.sum(jnp.where(row_id == col_id, work, 0.0), axis=1, keepdims=True)
    inverse = work[:, rank:] * lax.rsqrt(pivots)
    return jnp.dot(inverse, factor, precision=HIGHEST, preferred_element_type=F32)


def kernel(
    replicas, chunks,
    grad, error, moment, start_dirs, weight, norm_grads, gains,
    new_weight, new_error, new_moment, new_gains,
    grad_in, error_in, moment_in, dirs_in, moment_out, error_out, inputs, swapped, high, low,
    norm_send, norm_recv, factor_send, factor_recv, factor_all, dirs_send, dirs_recv, dirs_all,
    basis_own, basis_other, dirs_other,
    load_sem, store_sem, swap_send, swap_recv, norm_ssem, norm_rsem,
    fs_ssem, fs_rsem, fg_ssem, fg_rsem, ds_ssem, ds_rsem, dg_ssem, dg_rsem,
):
    me, core = lax.axis_index("dp"), lax.axis_index("tensor")
    other = 1 - core
    rows, width = inputs.shape[1:]
    rank = dirs_in.shape[0]
    piece_rows = rows // chunks

    def remote(src, dst, send_sem, recv_sem, to):
        return pltpu.make_async_remote_copy(
            src_ref=src, dst_ref=dst, send_sem=send_sem, recv_sem=recv_sem,
            device_id=to, device_id_type=pl.DeviceIdType.MESH,
        )

    def each_peer(body):
        def step(d, carry):
            body(d, lax.rem(me + d, replicas), lax.rem(me + replicas - d, replicas))
            return carry
        lax.fori_loop(1, replicas, step, 0)

    def scatter(send, recv, ssem, rsem):
        return lambda d, to, frm: remote(send.at[to], recv.at[d - 1], ssem.at[d - 1], rsem.at[d - 1], (to, core))

    def gather(full, ssem, rsem, receive=False):
        def copy(d, to, frm):
            slot = full.at[frm] if receive else full.at[me]
            return remote(slot, slot, ssem.at[d - 1], rsem.at[d - 1], (to, core))
        return copy

    def start(make):
        each_peer(lambda *a: make(*a).start())

    def wait_recv(make):
        each_peer(lambda *a: make(*a).wait_recv())

    def wait_send(make):
        each_peer(lambda *a: make(*a).wait_send())

    dirs_copy = pltpu.make_async_copy(start_dirs.at[core], dirs_in, load_sem.at[6 * chunks])
    loads = []
    for i, m in enumerate((other, core)):
        for c in range(chunks):
            r = pl.ds(c * piece_rows, piece_rows)
            loads.append([
                pltpu.make_async_copy(src.at[0, m, r], dst.at[m, r], load_sem.at[(i * chunks + c) * 3 + k])
                for k, (src, dst) in enumerate(((grad, grad_in), (moment, moment_in), (error, error_in)))
            ])
    for group in loads:
        for copy in group:
            copy.start()
    dirs_copy.start()

    barrier = pltpu.get_barrier_semaphore()
    each_peer(lambda d, to, frm: pl.semaphore_signal(
        barrier, inc=1, device_id=(to, core), device_id_type=pl.DeviceIdType.MESH))
    pl.semaphore_signal(barrier, inc=1, device_id=(me, other), device_id_type=pl.DeviceIdType.MESH)

    gain_cols = gains.shape[2]
    terms = norm_grads[0].astype(F32)
    for p in range(replicas):
        norm_send[p] = terms[:, p * gain_cols : (p + 1) * gain_cols]
    pl.semaphore_wait(barrier, replicas)

    swaps, stores = [], []
    for i, m in enumerate((other, core)):
        for c in range(chunks):
            for copy in loads[i * chunks + c]:
                copy.wait()

            @pl.loop(0, piece_rows // 16)
            def _(g):
                r = pl.ds(pl.multiple_of(c * piece_rows + g * 16, 16), 16)
                moment_f = momentum_decay * moment_in[m, r, :].astype(F32) + grad_in[m, r, :].astype(F32)
                moment_out[m, r, :] = moment_f.astype(BF16)
                x = moment_f + error_in[m, r, :].astype(F32)
                inputs[m, r, :] = x
                if i == 1:
                    high[core, r, :], low[core, r, :] = split(x)

            r = pl.ds(c * piece_rows, piece_rows)
            if i == 0:
                swaps.append(remote(inputs.at[m, r], swapped.at[r], swap_send.at[c], swap_recv.at[c], (me, other)))
                swaps[-1].start()
            stores.append(pltpu.make_async_copy(moment_out.at[m, r], new_moment.at[0, m, r], store_sem.at[i * chunks + c]))
            stores[-1].start()
    norm_copies = scatter(norm_send, norm_recv, norm_ssem, norm_rsem)
    start(norm_copies)
    dirs_copy.wait()
    for c in range(chunks):
        swaps[c].wait_recv()

        @pl.loop(0, piece_rows // 16)
        def _(g):
            r = pl.ds(pl.multiple_of(c * piece_rows + g * 16, 16), 16)
            high[other, r, :], low[other, r, :] = split(swapped[r, :])

    row_blocks = 2 * rows // LANES
    tiles = [(a, b) for a in range(rank // SUBLANES) for b in range(row_blocks)]

    def left(step, dirs):
        dirs_high, dirs_low = split(dirs)
        both = jnp.concatenate([dirs_high, dirs_low], axis=0)
        halves = []
        for h in range(2):
            part = dot_nt(both, high[h])
            halves.append(part[:rank] + part[rank:] + dot_nt(dirs_high, low[h]))
        factor = jnp.concatenate(halves, axis=1)
        send, recv, full = factor_send.at[step], factor_recv.at[step], factor_all.at[step]
        for j, (a, b) in enumerate(tiles):
            send[j] = factor[a * SUBLANES : (a + 1) * SUBLANES, b * LANES : (b + 1) * LANES]
        out = scatter(send, recv, fs_ssem.at[step], fs_rsem.at[step])
        start(out)
        wait_recv(out)
        total = send[me]
        for d in range(replicas - 1):
            total = total + recv[d]
        full[me] = total
        start(gather(full, fg_ssem.at[step], fg_rsem.at[step]))
        wait_recv(gather(full, fg_ssem.at[step], fg_rsem.at[step], True))
        return jnp.concatenate(
            [jnp.concatenate([full[a * row_blocks + b] for b in range(row_blocks)], axis=1) for a in range(rank // SUBLANES)],
            axis=0,
        )

    def right(step, basis):
        basis_high, basis_low = split(basis)
        both = jnp.concatenate([basis_high, basis_low], axis=0)
        send, recv, full = dirs_send.at[step], dirs_recv.at[step], dirs_all.at[step]
        span = min(width, 4 * LANES)
        for first in range(0, width, span):
            part = low_part = 0.0
            for h in range(2):
                part += jnp.dot(both[:, h * rows : (h + 1) * rows], high[h, :, first : first + span], preferred_element_type=F32)
                low_part += jnp.dot(basis_high[:, h * rows : (h + 1) * rows], low[h, :, first : first + span], preferred_element_type=F32)
            block = part[:rank] + part[rank:] + low_part
            for j in range(span // LANES):
                send[first // LANES + j] = block[:, j * LANES : (j + 1) * LANES]
        out = scatter(send, recv, ds_ssem.at[step], ds_rsem.at[step])
        start(out)
        wait_recv(out)
        total = send[me]
        for d in range(replicas - 1):
            total = total + recv[d]
        full[me] = total
        start(gather(full, dg_ssem.at[step], dg_rsem.at[step]))
        wait_recv(gather(full, dg_ssem.at[step], dg_rsem.at[step], True))

    right(0, basis_of(left(0, dirs_in[...])))
    full_dirs = jnp.concatenate([dirs_all[0, p] for p in range(replicas)], axis=1)
    basis = basis_of(left(1, full_dirs))
    basis_own[0], basis_own[1] = basis[:, :rows], basis[:, rows:]
    basis_swap = remote(basis_own.at[other], basis_other, swap_send.at[chunks], swap_recv.at[chunks], (me, other))
    basis_swap.start()
    right(1, basis)
    dirs_swap = remote(dirs_all.at[1], dirs_other, swap_send.at[chunks + 1], swap_recv.at[chunks + 1], (me, other))
    dirs_swap.start()

    def finish(m, basis_half, dirs):
        basis_high, basis_low = split(basis_half)
        lhs = jnp.concatenate([basis_high, basis_high, basis_low], axis=0)

        def approx_of(block):
            dirs_high, dirs_low = split(block)
            return dot_tn(lhs, jnp.concatenate([dirs_high, dirs_low, dirs_high], axis=0)) / replicas

        for first in range(0, replicas, 2):
            cols = slice(first * LANES, (first + 2) * LANES)
            approx = approx_of(jnp.concatenate([dirs[first], dirs[first + 1]], axis=1))
            error_out[m, :, cols] = (inputs[m, :, cols] - approx).astype(BF16)
        new_weight[m] = weight[m] - step_size * approx_of(dirs[me])

    def store_error(i, m):
        copy = pltpu.make_async_copy(error_out.at[m], new_error.at[0, m], store_sem.at[2 * chunks + i])
        copy.start()
        stores.append(copy)

    finish(core, basis_own[core], dirs_all.at[1])
    store_error(0, core)
    wait_recv(norm_copies)
    total = norm_send[me]
    for d in range(replicas - 1):
        total = total + norm_recv[d]
    for m in range(2):
        new_gains[m] = gains[m] - step_size * (total[m : m + 1] / replicas)
    basis_swap.wait_recv()
    dirs_swap.wait_recv()
    finish(other, basis_other[...], dirs_other)
    store_error(1, other)

    for copy in swaps + [basis_swap, dirs_swap]:
        copy.wait_send()
    wait_send(norm_copies)
    for s in range(2):
        wait_send(scatter(factor_send.at[s], factor_recv.at[s], fs_ssem.at[s], fs_rsem.at[s]))
        wait_send(gather(factor_all.at[s], fg_ssem.at[s], fg_rsem.at[s]))
        wait_send(scatter(dirs_send.at[s], dirs_recv.at[s], ds_ssem.at[s], ds_rsem.at[s]))
        wait_send(gather(dirs_all.at[s], dg_ssem.at[s], dg_rsem.at[s]))
    for copy in stores:
        copy.wait()


def kernel_shards(grad_kv, error_kv, moment_kv, start_dirs, weight_kv, norm_grads, norm_gains):
    replicas = lax.axis_size("dp")
    _, matrices, rows, width = grad_kv.shape
    rank = start_dirs.shape[1]
    gain_cols = norm_gains.shape[2]
    chunks = 2
    near = replicas - 1
    any_spec, vmem = pl.BlockSpec(memory_space=pl.ANY), pl.BlockSpec(memory_space=pltpu.VMEM)
    whole = (matrices, rows, width)
    dma = pltpu.SemaphoreType.DMA
    return pl.pallas_call(
        functools.partial(kernel, replicas, chunks),
        out_shape=(
            jax.ShapeDtypeStruct(weight_kv.shape, F32),
            jax.ShapeDtypeStruct(error_kv.shape, BF16),
            jax.ShapeDtypeStruct(moment_kv.shape, BF16),
            jax.ShapeDtypeStruct(norm_gains.shape, F32),
        ),
        in_specs=[any_spec] * 4 + [vmem] * 3,
        out_specs=(vmem, any_spec, any_spec, vmem),
        scratch_shapes=[
            pltpu.VMEM(whole, BF16), pltpu.VMEM(whole, BF16), pltpu.VMEM(whole, BF16),
            pltpu.VMEM((rank, width), F32), pltpu.VMEM(whole, BF16), pltpu.VMEM(whole, BF16),
            pltpu.VMEM(whole, F32), pltpu.VMEM((rows, width), F32),
            pltpu.VMEM(whole, BF16), pltpu.VMEM(whole, BF16),
            pltpu.VMEM((replicas, matrices, gain_cols), F32), pltpu.VMEM((near, matrices, gain_cols), F32),
            pltpu.VMEM((2, replicas, SUBLANES, LANES), F32), pltpu.VMEM((2, near, SUBLANES, LANES), F32),
            pltpu.VMEM((2, replicas, SUBLANES, LANES), F32),
            pltpu.VMEM((2, replicas, rank, LANES), F32), pltpu.VMEM((2, near, rank, LANES), F32),
            pltpu.VMEM((2, replicas, rank, LANES), F32),
            pltpu.VMEM((2, rank, rows), F32), pltpu.VMEM((rank, rows), F32),
            pltpu.VMEM((replicas, rank, LANES), F32),
            dma((6 * chunks + 1,)), dma((2 * chunks + 2,)), dma((chunks + 2,)), dma((chunks + 2,)),
            dma((near,)), dma((near,)),
        ] + [dma((2, near))] * 8,
        compiler_params=pltpu.CompilerParams(
            collective_id=0, has_side_effects=True, vmem_limit_bytes=44 * 2**20
        ),
        name="power_step",
    )(grad_kv, error_kv, moment_kv, start_dirs, weight_kv, norm_grads, norm_gains)


def solution(mesh):
    replicas, tensor = mesh.shape["dp"], mesh.shape["tensor"]

    def shards(*args):
        _, matrices, rows, width = args[0].shape
        rank = args[3].shape[1]
        fits = (
            tensor == matrices == 2
            and width == LANES * replicas
            and (rank // SUBLANES) * (2 * rows // LANES) == replicas
            and rank % SUBLANES == 0
            and rows % (2 * LANES) == 0
            and replicas % 2 == 0
        )
        return (kernel_shards if fits else plain_shards)(*args)

    return jax.shard_map(
        shards,
        mesh=mesh,
        in_specs=(
            P("dp", None, "tensor", None),
            P("dp", None, "tensor", None),
            P("dp", None, "tensor", None),
            P(),
            P(None, "tensor", "dp"),
            P("dp", None, "tensor"),
            P(None, "tensor", "dp"),
        ),
        out_specs=(
            P(None, "tensor", "dp"),
            P("dp", None, "tensor", None),
            P("dp", None, "tensor", None),
            P(None, "tensor", "dp"),
        ),
        check_vma=False,
    )
```

time: 541 us -> 81.7 us (0.15)
  waiting for transfers between devices: 415 us -> 0 us
  Pallas kernels: 0 us -> 70 us
  blocking collectives: 45 us -> 0 us
  matrix products: 35.5 us -> 0 us
  other arithmetic: 30.4 us -> 0 us
  between operations: 13.9 us -> 0.66 us
  local copies, waits for them, and re-layouts: 1.16 us -> 10.4 us
    psum x4 -> x0, waiting for transfers between devices: 415 us -> none  [the longest x2 213 us: column_sums(): summed = lax.psum(partial_sum, ('dp', 'tensor'))]
    pallas_call x0 -> x1, Pallas kernels: none -> 70 us  [kernel_shards(): pl.pallas_call(functools.partial(kernel, replicas, chunks), out_shape=(ja...]
    psum x1 -> x0, blocking collectives: 40.5 us -> none  [shards(): factor, norm_total = lax.psum((factor, norm_terms), 'dp')]
    dot_general x7 -> x0, matrix products: 33.3 us -> none  [the longest x2 15.7 us: project(): jnp.einsum('mrd,mkd->mrk', inputs, directions, precision=lax.Precision.HI...]
    another operation x12 -> x0, other arithmetic: 22 us -> none  [the longest x7 12 us: orthonormal(): cholesky_factor = jnp.linalg.cholesky(gram_matrix)]
    unnamed x14 -> x16, local copies, waits for them, and re-layouts: 1.01 us -> 10.4 us
  transfers between devices with their start and end apart: 4 -> 0, of which waited for: 4 -> 0; matrix products, arithmetic and copies ran while one was open for 1% -> 0% of each run, Pallas kernels for 0% -> 0%
where the time goes in v1:
time: 81.7 us; the launch traced here: 81 us
  Pallas kernels  70 us (86%)
  local copies, waits for them, and re-layouts  10.4 us (13%)
    pallas_call x1, Pallas kernels, kernel_shards(): pl.pallas_call(functools.partial(kernel, replicas, chunks), out_shape=(ja...  70 us
    unnamed x16, local copies, waits for them, and re-layouts  10.4 us

profile of v1, /device:TPU:0, one launch (start us, length us, event | category | flops | bytes accessed | tf_op | source)
XLA Modules:
  0.0 81.0 jit_solution(3567261717715370388)
XLA Ops:
  0.6 0.0 copy-start
  0.6 1.6 %copy-done = bf16[1,2,256,2048]{3,2,1,0:T(8,128)(2,1)S(1)} copy-done((bf16[1,2,256,2048]{3,2,1,0:T(8,128)(2,1)S(1)}, bf16[1,2,256,2048]{3,2,1,0:T(8,128)(2,1)}, u32[]{:S(2)}) %copy-start) | copy-done | bytes 2097176
  2.2 0.0 copy-start.1
  2.2 1.6 %copy-done.1 = bf16[1,2,256,2048]{3,2,1,0:T(8,128)(2,1)S(1)} copy-done((bf16[1,2,256,2048]{3,2,1,0:T(8,128)(2,1)S(1)}, bf16[1,2,256,2048]{3,2,1,0:T(8,128)(2,1)}, u32[]{:S(2)}) %copy-start.1) | copy-done | bytes 2097176
  3.8 0.0 copy-start.2
  3.8 1.0 %copy-done.2 = f32[2,32,2048]{2,1,0:T(8,128)S(1)} copy-done((f32[2,32,2048]{2,1,0:T(8,128)S(1)}, f32[2,32,2048]{2,1,0:T(8,128)}, u32[]{:S(2)}) %copy-start.2) | copy-done | bytes 524312
  4.9 0.0 copy-start.3
  4.9 0.9 %copy-done.3 = f32[2,256,128]{2,1,0:T(8,128)S(1)} copy-done((f32[2,256,128]{2,1,0:T(8,128)S(1)}, f32[2,256,128]{2,1,0:T(8,128)}, u32[]{:S(2)}) %copy-start.3) | copy-done | bytes 262168
  5.8 0.0 copy-start.4
  5.8 0.7 copy-done.4
  6.5 0.0 copy-start.5
  6.5 0.7 copy-done.5
  7.2 70.0 %power_step.1 = (f32[2,256,128]{2,1,0:T(8,128)S(1)}, bf16[1,2,256,2048]{3,2,1,0:T(8,128)(2,1)S(1)}, bf16[1,2,256,2048]{3,2,1,0:T(8,128)(2,1)S(1)}, f32[2,1,64]{2,1,0:T(1,128)S(1)}) custom-call(bf16[1,2,256,2048]{3,2,1,0:T(8,128)(2,1)S(1)} %copy-done, bf16[1,2,256,2048]{3,2,1,0:T(8,128)(2,1)S(1)} %copy-done.1, bf16[1,2,256,2048]{3,2,1,0:T(8,128)(2,1)} %moment.1, ...), custom_call_target="tpu_custom_call" | custom-call | tf_op jit(solution)/shard_map/power_step/pallas_call | solution.py:322
  77.1 0.7 copy.15
  77.8 1.3 %copy.16 = bf16[1,2,256,2048]{3,2,1,0:T(8,128)(2,1)} copy(bf16[1,2,256,2048]{3,2,1,0:T(8,128)(2,1)S(1)} %get-tuple-element.9) | data formatting | bytes 4194304
  79.2 1.3 %copy.17 = bf16[1,2,256,2048]{3,2,1,0:T(8,128)(2,1)} copy(bf16[1,2,256,2048]{3,2,1,0:T(8,128)(2,1)S(1)} %get-tuple-element.10) | data formatting | bytes 4194304
  80.5 0.6 copy.18
Async XLA Ops:
  0.6 1.6 %copy-start = (bf16[1,2,256,2048]{3,2,1,0:T(8,128)(2,1)S(1)}, bf16[1,2,256,2048]{3,2,1,0:T(8,128)(2,1)}, u32[]{:S(2)}) copy-start(bf16[1,2,256,2048]{3,2,1,0:T(8,128)(2,1)} %grad.1) | copy-start | bytes 6291460
  2.2 1.6 %copy-start.1 = (bf16[1,2,256,2048]{3,2,1,0:T(8,128)(2,1)S(1)}, bf16[1,2,256,2048]{3,2,1,0:T(8,128)(2,1)}, u32[]{:S(2)}) copy-start(bf16[1,2,256,2048]{3,2,1,0:T(8,128)(2,1)} %error.1) | copy-start | bytes 6291460
  3.8 1.0 %copy-start.2 = (f32[2,32,2048]{2,1,0:T(8,128)S(1)}, f32[2,32,2048]{2,1,0:T(8,128)}, u32[]{:S(2)}) copy-start(f32[2,32,2048]{2,1,0:T(8,128)} %start_dirs.1) | copy-start | bytes 1572868
  4.9 0.9 %copy-start.3 = (f32[2,256,128]{2,1,0:T(8,128)S(1)}, f32[2,256,128]{2,1,0:T(8,128)}, u32[]{:S(2)}) copy-start(f32[2,256,128]{2,1,0:T(8,128)} %weight.1) | copy-start | bytes 786436
  5.8 0.7 copy-start.4
  6.5 0.7 copy-start.5

commit v2 on v0

v2 whole, which is shorter than its diff:
```python
import functools

import jax
import jax.numpy as jnp
from jax import lax
from jax.experimental import pallas as pl
from jax.experimental.pallas import tpu as pltpu
from jax.sharding import PartitionSpec as P

momentum_decay = 0.9
step_size = 0.5
LANES = 128
SUBLANES = 8
F32 = jnp.float32
BF16 = jnp.bfloat16
HIGHEST = lax.Precision.HIGHEST


def project(inputs, directions):
    return jnp.einsum("mrd,mkd->mrk", inputs, directions, precision=HIGHEST)


def tri_solve(triangle, columns):
    return jax.scipy.linalg.solve_triangular(triangle, columns, lower=True)


def orthonormal(factor):
    full_rows = lax.all_gather(factor, "tensor", axis=1, tiled=True)
    gram_matrix = jnp.einsum("mrk,mrj->mkj", full_rows, full_rows, precision=HIGHEST)
    cholesky_factor = jnp.linalg.cholesky(gram_matrix)
    solved = jax.vmap(tri_solve)(cholesky_factor, jnp.swapaxes(factor, 1, 2))
    return jnp.swapaxes(solved, 1, 2)


def column_sums(inputs, basis):
    partial_sum = jnp.einsum("mrd,mrk->mkd", inputs, basis, precision=HIGHEST)
    return lax.psum(partial_sum, ("dp", "tensor"))


def plain_shards(grad_kv, error_kv, moment_kv, start_dirs, weight_kv, norm_grads, norm_gains):
    replicas = lax.axis_size("dp")
    dp_index = lax.axis_index("dp")
    moment_f = momentum_decay * moment_kv.astype(F32) + grad_kv.astype(F32)
    new_moment_kv = moment_f.astype(BF16)
    inputs = (moment_f + error_kv.astype(F32))[0]
    norm_terms = norm_grads[0].astype(F32)
    gain_cols = norm_gains.shape[2]
    factor = project(inputs, start_dirs)
    factor, norm_total = lax.psum((factor, norm_terms), "dp")
    own_norm = lax.dynamic_slice_in_dim(norm_total, dp_index * gain_cols, gain_cols, 1)
    mean_norm = own_norm / replicas
    basis = orthonormal(factor)
    directions = column_sums(inputs, basis)
    factor = lax.psum(project(inputs, directions), "dp")
    basis = orthonormal(factor)
    directions = column_sums(inputs, basis)
    approx = jnp.einsum("mrk,mkd->mrd", basis, directions, precision=HIGHEST) / replicas
    new_error_kv = (inputs - approx).astype(BF16)[None]
    weight_cols = weight_kv.shape[2]
    own_approx = lax.dynamic_slice_in_dim(approx, dp_index * weight_cols, weight_cols, 2)
    new_weight_kv = weight_kv - step_size * own_approx
    new_gains = norm_gains - step_size * mean_norm[:, None, :]
    return (new_weight_kv, new_error_kv, new_moment_kv, new_gains)


def split(value):
    high = value.astype(BF16)
    return high, (value - high.astype(F32)).astype(BF16)


def dot_nt(a, b):
    return lax.dot_general(a, b, (((1,), (1,)), ((), ())), preferred_element_type=F32)


def dot_tn(a, b):
    return lax.dot_general(a, b, (((0,), (0,)), ((), ())), preferred_element_type=F32)


def basis_of(factor, block=8):
    rank = factor.shape[0]
    gram = lax.dot_general(
        factor, factor, (((1,), (1,)), ((), ())), precision=HIGHEST, preferred_element_type=F32
    )
    row_id = lax.broadcasted_iota(jnp.int32, (rank, 2 * rank), 0)
    col_id = lax.broadcasted_iota(jnp.int32, (rank, 2 * rank), 1)
    unit = (lax.broadcasted_iota(jnp.int32, (rank, rank), 0) == lax.broadcasted_iota(jnp.int32, (rank, rank), 1)).astype(F32)
    work = jnp.concatenate([gram, unit], axis=1)
    for first in range(0, rank, block):
        cols = [jnp.broadcast_to(work[:, j : j + 1], work.shape) for j in range(first, first + block)]
        rows = [work[j : j + 1, :] for j in range(first, first + block)]
        for i in range(block):
            j = first + i
            ratio = jnp.where(row_id > j, cols[i] / cols[i][j : j + 1, :], 0.0)
            for k in range(i + 1, block):
                cols[k] = cols[k] - ratio * cols[k][j : j + 1, :]
                rows[k] = rows[k] - ratio[first + k : first + k + 1, :] * rows[i]
            work = work - ratio * rows[i]
    pivots = jnp.sum(jnp.where(row_id == col_id, work, 0.0), axis=1, keepdims=True)
    inverse = work[:, rank:] * lax.rsqrt(pivots)
    return jnp.dot(inverse, factor, precision=HIGHEST, preferred_element_type=F32)


def kernel(
    outer, inner, chunks,
    grad, error, moment, start_dirs, weight, norm_grads, gains,
    new_weight, new_error, new_moment, new_gains,
    grad_in, error_in, moment_in, dirs_in, weight_in, norm_in, gains_in, inputs, swapped, high, low,
    norm_send, norm_recv, norm_part, norm_far,
    first_send, first_recv, factor_send, factor_near, factor_far, factor_all,
    dirs_send, dirs_near, dirs_part, dirs_far, dirs_all, basis_own, basis_other, dirs_other,
    load_sem, swap_ssem, swap_rsem, norm_ssem, norm_rsem, factor_ssem, factor_rsem, dirs_ssem, dirs_rsem,
):
    me, core = lax.axis_index("dp"), lax.axis_index("tensor")
    other = 1 - core
    far, near = lax.div(me, inner), lax.rem(me, inner)
    replicas = outer * inner
    rows, width = inputs.shape[1:]
    rank = dirs_in.shape[1]
    piece_rows = rows // chunks
    span = width // outer
    sends = []

    def remote(src, dst, send_sem, recv_sem, to):
        return pltpu.make_async_remote_copy(
            src_ref=src, dst_ref=dst, send_sem=send_sem, recv_sem=recv_sem,
            device_id=to, device_id_type=pl.DeviceIdType.MESH,
        )

    def send(*args):
        copy = remote(*args)
        copy.start()
        sends.append(copy)
        return copy

    def near_at(d):
        return lax.rem(near + d + inner, inner)

    def far_at(d):
        return lax.rem(far + d + outer, outer)

    def near_peer(d):
        return (far * inner + near_at(d), core)

    def far_peer(d):
        return (far_at(d) * inner + near, core)

    def columns(z):
        return pl.ds(pl.multiple_of(z * span, span), span)

    last = 6 * chunks
    small = [
        pltpu.make_async_copy(src, dst, load_sem.at[last + k])
        for k, (src, dst) in enumerate(((start_dirs, dirs_in), (norm_grads, norm_in), (weight, weight_in), (gains, gains_in)))
    ]
    loads = []
    for i, m in enumerate((other, core)):
        for c in range(chunks):
            r = pl.ds(c * piece_rows, piece_rows)
            loads.append([
                pltpu.make_async_copy(src.at[0, m, r], dst.at[m, r], load_sem.at[(i * chunks + c) * 3 + k])
                for k, (src, dst) in enumerate(((grad, grad_in), (moment, moment_in), (error, error_in)))
            ])
    for n, group in enumerate(loads):
        for copy in group:
            copy.start()
        if n == 0:
            small[0].start()
            small[1].start()
    small[2].start()
    small[3].start()

    barrier = pltpu.get_barrier_semaphore()
    greeted = [near_peer(d) for d in range(1, inner)] + [far_peer(d) for d in range(1, outer)] + [(me, other)]
    for device in greeted:
        pl.semaphore_signal(barrier, inc=1, device_id=device, device_id_type=pl.DeviceIdType.MESH)

    def form(i, m):
        for c in range(chunks):
            for copy in loads[i * chunks + c]:
                copy.wait()

            @pl.loop(0, piece_rows // 16)
            def _(g):
                r = pl.ds(pl.multiple_of(c * piece_rows + g * 16, 16), 16)
                moment_f = momentum_decay * moment_in[m, r, :].astype(F32) + grad_in[m, r, :].astype(F32)
                new_moment[0, m, r, :] = moment_f.astype(BF16)
                x = moment_f + error_in[m, r, :].astype(F32)
                inputs[m, r, :] = x
                high[m, r, :], low[m, r, :] = split(x)

    def left_of(dirs, h, cols=slice(None)):
        dirs_high, dirs_low = split(dirs)
        part = dot_nt(jnp.concatenate([dirs_high, dirs_low], axis=0), high[h, :, cols])
        return part[:rank] + part[rank:] + dot_nt(dirs_high, low[h, :, cols])

    def left_sum(step, factor, between=None):
        block = rank // inner
        own, arrived, summed, full = factor_send.at[step], factor_near.at[step], factor_far.at[step], factor_all.at[step]
        ssem, rsem = factor_ssem.at[step], factor_rsem.at[step]
        for q in range(inner):
            own[q] = factor[q * block : (q + 1) * block, :]
        waits = [send(own.at[near_at(d)], arrived.at[d - 1], ssem.at[d - 1], rsem.at[d - 1], near_peer(d)) for d in range(1, inner)]
        if between is not None:
            between()
        total = own[near]
        for d in range(1, inner):
            waits[d - 1].wait_recv()
            total = total + arrived[d - 1]
        summed[far] = total
        base = inner - 1
        for d in range(1, outer):
            send(summed.at[far], summed.at[far], ssem.at[base + d - 1], rsem.at[base + d - 1], far_peer(d))
        for d in range(1, outer):
            slot = summed.at[far_at(-d)]
            remote(slot, slot, ssem.at[base + d - 1], rsem.at[base + d - 1], far_peer(d)).wait_recv()
        total = summed[0]
        for z in range(1, outer):
            total = total + summed[z]
        full[near] = total
        base += outer - 1
        for d in range(1, inner):
            send(full.at[near], full.at[near], ssem.at[base + d - 1], rsem.at[base + d - 1], near_peer(d))
        for d in range(1, inner):
            slot = full.at[near_at(-d)]
            remote(slot, slot, ssem.at[base + d - 1], rsem.at[base + d - 1], near_peer(d)).wait_recv()
        return jnp.concatenate([full[q] for q in range(inner)], axis=0)

    def right_sum(step, basis, consume):
        basis_high, basis_low = split(basis)
        both = jnp.concatenate([basis_high, basis_low], axis=0)
        own, arrived, part, other_far, full = (
            dirs_send.at[step], dirs_near.at[step], dirs_part.at[step], dirs_far.at[step], dirs_all.at[step]
        )
        ssem, rsem = dirs_ssem.at[step], dirs_rsem.at[step]
        order = list(range(1, outer)) + [0]
        waits = {}
        for dz in order:
            z = far_at(dz)
            sums = low_sums = 0.0
            for h in range(2):
                half = slice(h * rows, (h + 1) * rows)
                sums += jnp.dot(both[:, half], high[h, :, columns(z)], preferred_element_type=F32)
                low_sums += jnp.dot(basis_high[:, half], low[h, :, columns(z)], preferred_element_type=F32)
            block = sums[:rank] + sums[rank:] + low_sums
            for q in range(inner):
                own[z, q] = block[:, q * LANES : (q + 1) * LANES]
            for d in range(1, inner):
                k = dz * (inner - 1) + d - 1
                waits[dz, d] = send(own.at[z, near_at(d)], arrived.at[z, d - 1], ssem.at[k], rsem.at[k], near_peer(d))
        base = outer * (inner - 1)
        far_waits = []
        for dz in order:
            z = far_at(dz)
            total = own[z, near]
            for d in range(1, inner):
                waits[dz, d].wait_recv()
                total = total + arrived[z, d - 1]
            if dz:
                part[z] = total
                k = base + dz - 1
                far_waits.append(send(part.at[z], other_far.at[dz - 1], ssem.at[k], rsem.at[k], far_peer(dz)))
        for dz in range(1, outer):
            far_waits[dz - 1].wait_recv()
            total = total + other_far[dz - 1]
        full[far, near] = total
        base += outer - 1
        for dz in range(1, outer):
            k = base + dz - 1
            send(full.at[far, near], full.at[far, near], ssem.at[k], rsem.at[k], far_peer(dz))
        spread = base + outer - 1

        def forward(dz):
            for d in range(1, inner):
                k = spread + dz * (inner - 1) + d - 1
                slot = full.at[far_at(-dz), near]
                send(slot, slot, ssem.at[k], rsem.at[k], near_peer(d))

        def take(dz):
            z = far_at(-dz)
            for d in range(1, inner):
                k = spread + dz * (inner - 1) + d - 1
                slot = full.at[z, near_at(-d)]
                remote(slot, slot, ssem.at[k], rsem.at[k], near_peer(d)).wait_recv()
            consume(dz, z, jnp.concatenate([full[z, q] for q in range(inner)], axis=1))

        forward(0)
        for dz in range(1, outer):
            slot = full.at[far_at(-dz), near]
            remote(slot, slot, ssem.at[base + dz - 1], rsem.at[base + dz - 1], far_peer(dz)).wait_recv()
            forward(dz)
            take(dz - 1)
        take(outer - 1)

    form(0, other)
    small[0].wait()
    first_send[...] = left_of(dirs_in[other], other)
    pl.semaphore_wait(barrier, len(greeted))
    first_swap = send(first_send, first_recv, swap_ssem.at[0], swap_rsem.at[0], (me, other))
    matrix_swap = send(inputs.at[other], swapped, swap_ssem.at[1], swap_rsem.at[1], (me, other))
    form(1, core)
    own_left = left_of(dirs_in[core], core)

    small[1].wait()
    gain_cols = gains.shape[2]
    terms = norm_in[0].astype(F32)
    for z in range(outer):
        for q in range(inner):
            p = z * inner + q
            norm_send[q, z] = terms[:, p * gain_cols : (p + 1) * gain_cols]

    first_swap.wait_recv()
    their_left = first_recv[...]
    factor = jnp.concatenate([
        jnp.where(core == 0, own_left, their_left), jnp.where(core == 0, their_left, own_left)
    ], axis=1)

    norm_waits, norm_far_waits = [], []

    def while_summing():
        for d in range(1, inner):
            norm_waits.append(send(norm_send.at[near_at(d)], norm_recv.at[d - 1], norm_ssem.at[d - 1], norm_rsem.at[d - 1], near_peer(d)))
        matrix_swap.wait_recv()

        @pl.loop(0, rows // 16)
        def _(g):
            r = pl.ds(pl.multiple_of(g * 16, 16), 16)
            high[other, r, :], low[other, r, :] = split(swapped[r, :])

    basis = basis_of(left_sum(0, factor, while_summing))

    halves = [jnp.zeros((rank, rows), F32), jnp.zeros((rank, rows), F32)]

    def add_left(dz, z, block):
        for h in range(2):
            halves[h] = halves[h] + left_of(block, h, columns(z))

    right_sum(0, basis, add_left)

    def norm_step():
        total = norm_send[near]
        for d in range(1, inner):
            norm_waits[d - 1].wait_recv()
            total = total + norm_recv[d - 1]
        norm_part[...] = total
        for d in range(1, outer):
            k = inner - 1 + d - 1
            norm_far_waits.append(send(norm_part.at[far_at(d)], norm_far.at[d - 1], norm_ssem.at[k], norm_rsem.at[k], far_peer(d)))

    basis = basis_of(left_sum(1, jnp.concatenate(halves, axis=1), norm_step))
    basis_own[0], basis_own[1] = basis[:, :rows], basis[:, rows:]
    basis_swap = send(basis_own.at[other], basis_other, swap_ssem.at[2], swap_rsem.at[2], (me, other))

    def left_side(half):
        basis_high, basis_low = split(half)
        return jnp.concatenate([basis_high, basis_high, basis_low], axis=0)

    def approx_of(lhs, block):
        dirs_high, dirs_low = split(block)
        return dot_tn(lhs, jnp.concatenate([dirs_high, dirs_low, dirs_high], axis=0)) / replicas

    def finish(m, lhs, z, block):
        new_error[0, m, :, columns(z)] = (inputs[m, :, columns(z)] - approx_of(lhs, block)).astype(BF16)

    dirs_waits = []
    own_side = left_side(basis_own[core])

    def use_own(dz, z, block):
        k = 3 + dz
        dirs_waits.append(send(dirs_all.at[1, z], dirs_other.at[z], swap_ssem.at[k], swap_rsem.at[k], (me, other)))
        finish(core, own_side, z, block)

    right_sum(1, basis, use_own)
    small[2].wait()
    small[3].wait()
    new_weight[core] = weight_in[core] - step_size * approx_of(own_side, dirs_all[1, far, near])
    total = norm_part[far]
    for d in range(1, outer):
        norm_far_waits[d - 1].wait_recv()
        total = total + norm_far[d - 1]
    for m in range(2):
        new_gains[m] = gains_in[m] - step_size * (total[m : m + 1] / replicas)
    basis_swap.wait_recv()
    other_side = left_side(basis_other[...])
    for dz in range(outer):
        z = far_at(-dz)
        dirs_waits[dz].wait_recv()
        finish(other, other_side, z, jnp.concatenate([dirs_other[z, q] for q in range(inner)], axis=1))
    new_weight[other] = weight_in[other] - step_size * approx_of(other_side, dirs_other[far, near])

    for copy in sends:
        copy.wait_send()


def levels(replicas):
    near = max(d for d in range(1, replicas + 1) if replicas % d == 0 and d * d <= replicas)
    return replicas // near, near


def kernel_shards(grad_kv, error_kv, moment_kv, start_dirs, weight_kv, norm_grads, norm_gains):
    outer, inner = levels(lax.axis_size("dp"))
    _, matrices, rows, width = grad_kv.shape
    rank = start_dirs.shape[1]
    gain_cols = norm_gains.shape[2]
    chunks = 2
    hbm, vmem = pl.BlockSpec(memory_space=pltpu.HBM), pl.BlockSpec(memory_space=pltpu.VMEM)
    whole = (matrices, rows, width)
    block = rank // inner
    dma = pltpu.SemaphoreType.DMA
    factor_copies = 2 * (inner - 1) + outer - 1
    dirs_copies = 2 * outer * (inner - 1) + 2 * (outer - 1)
    return pl.pallas_call(
        functools.partial(kernel, outer, inner, chunks),
        out_shape=(
            jax.ShapeDtypeStruct(weight_kv.shape, F32),
            jax.ShapeDtypeStruct(error_kv.shape, BF16),
            jax.ShapeDtypeStruct(moment_kv.shape, BF16),
            jax.ShapeDtypeStruct(norm_gains.shape, F32),
        ),
        in_specs=[hbm] * 7,
        out_specs=(vmem,) * 4,
        scratch_shapes=[
            pltpu.VMEM(whole, BF16), pltpu.VMEM(whole, BF16), pltpu.VMEM(whole, BF16),
            pltpu.VMEM(start_dirs.shape, F32), pltpu.VMEM(weight_kv.shape, F32),
            pltpu.VMEM(norm_grads.shape, BF16), pltpu.VMEM(norm_gains.shape, F32),
            pltpu.VMEM(whole, F32), pltpu.VMEM((rows, width), F32),
            pltpu.VMEM(whole, BF16), pltpu.VMEM(whole, BF16),
            pltpu.VMEM((inner, outer, matrices, gain_cols), F32), pltpu.VMEM((inner - 1, outer, matrices, gain_cols), F32),
            pltpu.VMEM((outer, matrices, gain_cols), F32), pltpu.VMEM((outer - 1, matrices, gain_cols), F32),
            pltpu.VMEM((rank, rows), F32), pltpu.VMEM((rank, rows), F32),
            pltpu.VMEM((2, inner, block, 2 * rows), F32), pltpu.VMEM((2, inner - 1, block, 2 * rows), F32),
            pltpu.VMEM((2, outer, block, 2 * rows), F32), pltpu.VMEM((2, inner, block, 2 * rows), F32),
            pltpu.VMEM((2, outer, inner, rank, LANES), F32), pltpu.VMEM((2, outer, inner - 1, rank, LANES), F32),
            pltpu.VMEM((2, outer, rank, LANES), F32), pltpu.VMEM((2, outer - 1, rank, LANES), F32),
            pltpu.VMEM((2, outer, inner, rank, LANES), F32),
            pltpu.VMEM((2, rank, rows), F32), pltpu.VMEM((rank, rows), F32),
            pltpu.VMEM((outer, inner, rank, LANES), F32),
            dma((6 * chunks + 4,)), dma((3 + outer,)), dma((3 + outer,)),
            dma((inner + outer - 2,)), dma((inner + outer - 2,)),
            dma((2, factor_copies)), dma((2, factor_copies)), dma((2, dirs_copies)), dma((2, dirs_copies)),
        ],
        compiler_params=pltpu.CompilerParams(
            collective_id=0, has_side_effects=True, vmem_limit_bytes=44 * 2**20
        ),
        name="power_step",
    )(grad_kv, error_kv, moment_kv, start_dirs, weight_kv, norm_grads, norm_gains)


def solution(mesh):
    replicas, tensor = mesh.shape["dp"], mesh.shape["tensor"]

    def shards(*args):
        _, matrices, rows, width = args[0].shape
        rank = args[3].shape[1]
        _, near = levels(replicas)
        fits = (
            tensor == matrices == 2
            and near > 1
            and width == LANES * replicas
            and rank % (SUBLANES * near) == 0
            and rows % (2 * LANES) == 0
        )
        return (kernel_shards if fits else plain_shards)(*args)

    return jax.shard_map(
        shards,
        mesh=mesh,
        in_specs=(
            P("dp", None, "tensor", None),
            P("dp", None, "tensor", None),
            P("dp", None, "tensor", None),
            P(),
            P(None, "tensor", "dp"),
            P("dp", None, "tensor"),
            P(None, "tensor", "dp"),
        ),
        out_specs=(
            P(None, "tensor", "dp"),
            P("dp", None, "tensor", None),
            P("dp", None, "tensor", None),
            P(None, "tensor", "dp"),
        ),
        check_vma=False,
    )
```

time: 541 us -> 82.6 us (0.15)
  waiting for transfers between devices: 415 us -> 0 us
  Pallas kernels: 0 us -> 71.2 us
  blocking collectives: 45 us -> 0 us
  matrix products: 35.5 us -> 0 us
  other arithmetic: 30.4 us -> 0 us
  between operations: 13.9 us -> 0.66 us
  local copies, waits for them, and re-layouts: 1.16 us -> 10.4 us
    psum x4 -> x0, waiting for transfers between devices: 415 us -> none  [the longest x2 213 us: column_sums(): summed = lax.psum(partial_sum, ('dp', 'tensor'))]
    pallas_call x0 -> x1, Pallas kernels: none -> 71.2 us  [kernel_shards(): pl.pallas_call(functools.partial(kernel, outer, inner, chunks), out_shape...]
    psum x1 -> x0, blocking collectives: 40.5 us -> none  [shards(): factor, norm_total = lax.psum((factor, norm_terms), 'dp')]
    dot_general x7 -> x0, matrix products: 33.3 us -> none  [the longest x2 15.7 us: project(): jnp.einsum('mrd,mkd->mrk', inputs, directions, precision=lax.Precision.HI...]
    another operation x12 -> x0, other arithmetic: 22 us -> none  [the longest x7 12 us: orthonormal(): cholesky_factor = jnp.linalg.cholesky(gram_matrix)]
    unnamed x14 -> x16, local copies, waits for them, and re-layouts: 1.01 us -> 10.4 us
  transfers between devices with their start and end apart: 4 -> 0, of which waited for: 4 -> 0; matrix products, arithmetic and copies ran while one was open for 1% -> 0% of each run, Pallas kernels for 0% -> 0%
where the time goes in v2:
time: 82.6 us; the launch traced here: 82.3 us
  Pallas kernels  71.2 us (86%)
  local copies, waits for them, and re-layouts  10.4 us (13%)
    pallas_call x1, Pallas kernels, kernel_shards(): pl.pallas_call(functools.partial(kernel, outer, inner, chunks), out_shape...  71.2 us
    unnamed x16, local copies, waits for them, and re-layouts  10.4 us

profile of v2, /device:TPU:0, one launch (start us, length us, event | category | flops | bytes accessed | tf_op | source)
XLA Modules:
  0.0 82.3 jit_solution(5019022443359931966)
XLA Ops:
  0.6 0.0 copy-start
  0.6 1.6 %copy-done = bf16[1,2,256,2048]{3,2,1,0:T(8,128)(2,1)S(1)} copy-done((bf16[1,2,256,2048]{3,2,1,0:T(8,128)(2,1)S(1)}, bf16[1,2,256,2048]{3,2,1,0:T(8,128)(2,1)}, u32[]{:S(2)}) %copy-start) | copy-done | bytes 2097176
  2.2 0.0 copy-start.1
  2.2 1.6 %copy-done.1 = bf16[1,2,256,2048]{3,2,1,0:T(8,128)(2,1)S(1)} copy-done((bf16[1,2,256,2048]{3,2,1,0:T(8,128)(2,1)S(1)}, bf16[1,2,256,2048]{3,2,1,0:T(8,128)(2,1)}, u32[]{:S(2)}) %copy-start.1) | copy-done | bytes 2097176
  3.8 0.0 copy-start.2
  3.8 1.0 %copy-done.2 = f32[2,32,2048]{2,1,0:T(8,128)S(1)} copy-done((f32[2,32,2048]{2,1,0:T(8,128)S(1)}, f32[2,32,2048]{2,1,0:T(8,128)}, u32[]{:S(2)}) %copy-start.2) | copy-done | bytes 524312
  4.9 0.0 copy-start.3
  4.9 0.9 %copy-done.3 = f32[2,256,128]{2,1,0:T(8,128)S(1)} copy-done((f32[2,256,128]{2,1,0:T(8,128)S(1)}, f32[2,256,128]{2,1,0:T(8,128)}, u32[]{:S(2)}) %copy-start.3) | copy-done | bytes 262168
  5.8 0.0 copy-start.4
  5.8 0.7 copy-done.4
  6.5 0.0 copy-start.5
  6.5 0.7 copy-done.5
  7.2 71.2 %power_step.1 = (f32[2,256,128]{2,1,0:T(8,128)S(1)}, bf16[1,2,256,2048]{3,2,1,0:T(8,128)(2,1)S(1)}, bf16[1,2,256,2048]{3,2,1,0:T(8,128)(2,1)S(1)}, f32[2,1,64]{2,1,0:T(1,128)S(1)}) custom-call(bf16[1,2,256,2048]{3,2,1,0:T(8,128)(2,1)S(1)} %copy-done, bf16[1,2,256,2048]{3,2,1,0:T(8,128)(2,1)S(1)} %copy-done.1, bf16[1,2,256,2048]{3,2,1,0:T(8,128)(2,1)} %moment.1, ...), custom_call_target="tpu_custom_call" | custom-call | tf_op jit(solution)/shard_map/power_step/pallas_call | solution.py:411
  78.4 0.7 copy.15
  79.1 1.3 %copy.16 = bf16[1,2,256,2048]{3,2,1,0:T(8,128)(2,1)} copy(bf16[1,2,256,2048]{3,2,1,0:T(8,128)(2,1)S(1)} %get-tuple-element.9) | data formatting | bytes 4194304
  80.4 1.3 %copy.17 = bf16[1,2,256,2048]{3,2,1,0:T(8,128)(2,1)} copy(bf16[1,2,256,2048]{3,2,1,0:T(8,128)(2,1)S(1)} %get-tuple-element.10) | data formatting | bytes 4194304
  81.7 0.6 copy.18
Async XLA Ops:
  0.6 1.6 %copy-start = (bf16[1,2,256,2048]{3,2,1,0:T(8,128)(2,1)S(1)}, bf16[1,2,256,2048]{3,2,1,0:T(8,128)(2,1)}, u32[]{:S(2)}) copy-start(bf16[1,2,256,2048]{3,2,1,0:T(8,128)(2,1)} %grad.1) | copy-start | bytes 6291460
  2.2 1.6 %copy-start.1 = (bf16[1,2,256,2048]{3,2,1,0:T(8,128)(2,1)S(1)}, bf16[1,2,256,2048]{3,2,1,0:T(8,128)(2,1)}, u32[]{:S(2)}) copy-start(bf16[1,2,256,2048]{3,2,1,0:T(8,128)(2,1)} %error.1) | copy-start | bytes 6291460
  3.8 1.0 %copy-start.2 = (f32[2,32,2048]{2,1,0:T(8,128)S(1)}, f32[2,32,2048]{2,1,0:T(8,128)}, u32[]{:S(2)}) copy-start(f32[2,32,2048]{2,1,0:T(8,128)} %start_dirs.1) | copy-start | bytes 1572868
  4.9 0.9 %copy-start.3 = (f32[2,256,128]{2,1,0:T(8,128)S(1)}, f32[2,256,128]{2,1,0:T(8,128)}, u32[]{:S(2)}) copy-start(f32[2,256,128]{2,1,0:T(8,128)} %weight.1) | copy-start | bytes 786436
  5.8 0.7 copy-start.4
  6.5 0.7 copy-start.5

commit v3 on v2

--- a/solution.py
+++ b/solution.py
@@ -90,7 +90,7 @@
         rows = [work[j : j + 1, :] for j in range(first, first + block)]
         for i in range(block):
             j = first + i
-            ratio = jnp.where(row_id > j, cols[i] / cols[i][j : j + 1, :], 0.0)
+            ratio = jnp.where(row_id > j, cols[i] * (1.0 / cols[i][j : j + 1, :]), 0.0)
             for k in range(i + 1, block):
                 cols[k] = cols[k] - ratio * cols[k][j : j + 1, :]
                 rows[k] = rows[k] - ratio[first + k : first + k + 1, :] * rows[i]
@@ -102,13 +102,13 @@
 
 def kernel(
     outer, inner, chunks,
-    grad, error, moment, start_dirs, weight, norm_grads, gains,
-    new_weight, new_error, new_moment, new_gains,
-    grad_in, error_in, moment_in, dirs_in, weight_in, norm_in, gains_in, inputs, swapped, high, low,
+    grad, error, moment, start_dirs, norm_grads,
+    own_approx, new_error, new_moment, mean_norm,
+    grad_in, error_in, moment_in, dirs_in, norm_in, moment_out, error_out, inputs, swapped, high, low,
     norm_send, norm_recv, norm_part, norm_far,
-    first_send, first_recv, factor_send, factor_near, factor_far, factor_all,
+    first_send, first_recv, factor_send, factor_recv, factor_all,
     dirs_send, dirs_near, dirs_part, dirs_far, dirs_all, basis_own, basis_other, dirs_other,
-    load_sem, swap_ssem, swap_rsem, norm_ssem, norm_rsem, factor_ssem, factor_rsem, dirs_ssem, dirs_rsem,
+    load_sem, store_sem, swap_ssem, swap_rsem, norm_ssem, norm_rsem, factor_ssem, factor_rsem, dirs_ssem, dirs_rsem,
 ):
     me, core = lax.axis_index("dp"), lax.axis_index("tensor")
     other = 1 - core
@@ -118,7 +118,12 @@
     rank = dirs_in.shape[1]
     piece_rows = rows // chunks
     span = width // outer
-    sends = []
+    sends, stores = [], []
+
+    def store(src, dst):
+        copy = pltpu.make_async_copy(src, dst, store_sem.at[len(stores)])
+        copy.start()
+        stores.append(copy)
 
     def remote(src, dst, send_sem, recv_sem, to):
         return pltpu.make_async_remote_copy(
@@ -144,13 +149,16 @@
     def far_peer(d):
         return (far_at(d) * inner + near, core)
 
+    def peer(d):
+        return (lax.rem(me + d + replicas, replicas), core)
+
     def columns(z):
         return pl.ds(pl.multiple_of(z * span, span), span)
 
     last = 6 * chunks
     small = [
         pltpu.make_async_copy(src, dst, load_sem.at[last + k])
-        for k, (src, dst) in enumerate(((start_dirs, dirs_in), (norm_grads, norm_in), (weight, weight_in), (gains, gains_in)))
+        for k, (src, dst) in enumerate(((start_dirs, dirs_in), (norm_grads, norm_in)))
     ]
     loads = []
     for i, m in enumerate((other, core)):
@@ -166,11 +174,9 @@
         if n == 0:
             small[0].start()
             small[1].start()
-    small[2].start()
-    small[3].start()
 
     barrier = pltpu.get_barrier_semaphore()
-    greeted = [near_peer(d) for d in range(1, inner)] + [far_peer(d) for d in range(1, outer)] + [(me, other)]
+    greeted = [peer(d) for d in range(1, replicas)] + [(me, other)]
     for device in greeted:
         pl.semaphore_signal(barrier, inc=1, device_id=device, device_id_type=pl.DeviceIdType.MESH)
 
@@ -183,10 +189,12 @@
             def _(g):
                 r = pl.ds(pl.multiple_of(c * piece_rows + g * 16, 16), 16)
                 moment_f = momentum_decay * moment_in[m, r, :].astype(F32) + grad_in[m, r, :].astype(F32)
-                new_moment[0, m, r, :] = moment_f.astype(BF16)
+                moment_out[m, r, :] = moment_f.astype(BF16)
                 x = moment_f + error_in[m, r, :].astype(F32)
                 inputs[m, r, :] = x
                 high[m, r, :], low[m, r, :] = split(x)
+
+        store(moment_out.at[m], new_moment.at[0, m])
 
     def left_of(dirs, h, cols=slice(None)):
         dirs_high, dirs_low = split(dirs)
@@ -194,36 +202,35 @@
         return part[:rank] + part[rank:] + dot_nt(dirs_high, low[h, :, cols])
 
     def left_sum(step, factor, between=None):
-        block = rank // inner
-        own, arrived, summed, full = factor_send.at[step], factor_near.at[step], factor_far.at[step], factor_all.at[step]
+        own, arrived, full = factor_send.at[step], factor_recv.at[step], factor_all.at[step]
         ssem, rsem = factor_ssem.at[step], factor_rsem.at[step]
-        for q in range(inner):
-            own[q] = factor[q * block : (q + 1) * block, :]
-        waits = [send(own.at[near_at(d)], arrived.at[d - 1], ssem.at[d - 1], rsem.at[d - 1], near_peer(d)) for d in range(1, inner)]
+        row_blocks = 2 * rows // LANES
+        for j in range(replicas):
+            a, b = divmod(j, row_blocks)
+            own[j] = factor[a * SUBLANES : (a + 1) * SUBLANES, b * LANES : (b + 1) * LANES]
+        order = sorted(range(1, replicas), key=lambda d: abs(2 * d - replicas))
+        waits = [send(own.at[peer(d)[0]], arrived.at[d - 1], ssem.at[d - 1], rsem.at[d - 1], peer(d)) for d in order]
         if between is not None:
             between()
-        total = own[near]
-        for d in range(1, inner):
-            waits[d - 1].wait_recv()
+        for copy in waits:
+            copy.wait_recv()
+        total = own[me]
+        for d in range(1, replicas):
             total = total + arrived[d - 1]
-        summed[far] = total
-        base = inner - 1
-        for d in range(1, outer):
-            send(summed.at[far], summed.at[far], ssem.at[base + d - 1], rsem.at[base + d - 1], far_peer(d))
-        for d in range(1, outer):
-            slot = summed.at[far_at(-d)]
-            remote(slot, slot, ssem.at[base + d - 1], rsem.at[base + d - 1], far_peer(d)).wait_recv()
-        total = summed[0]
-        for z in range(1, outer):
-            total = total + summed[z]
-        full[near] = total
-        base += outer - 1
-        for d in range(1, inner):
-            send(full.at[near], full.at[near], ssem.at[base + d - 1], rsem.at[base + d - 1], near_peer(d))
-        for d in range(1, inner):
-            slot = full.at[near_at(-d)]
-            remote(slot, slot, ssem.at[base + d - 1], rsem.at[base + d - 1], near_peer(d)).wait_recv()
-        return jnp.concatenate([full[q] for q in range(inner)], axis=0)
+        full[me] = total
+        base = replicas - 1
+        for d in order:
+            send(full.at[me], full.at[me], ssem.at[base + d - 1], rsem.at[base + d - 1], peer(d))
+        for d in order:
+            slot = full.at[peer(-d)[0]]
+            remote(slot, slot, ssem.at[base + d - 1], rsem.at[base + d - 1], peer(d)).wait_recv()
+        return jnp.concatenate(
+            [
+                jnp.concatenate([full[a * row_blocks + b] for b in range(row_blocks)], axis=1)
+                for a in range(rank // SUBLANES)
+            ],
+            axis=0,
+        )
 
     def right_sum(step, basis, consume):
         basis_high, basis_low = split(basis)
@@ -301,7 +308,7 @@
     own_left = left_of(dirs_in[core], core)
 
     small[1].wait()
-    gain_cols = gains.shape[2]
+    gain_cols = mean_norm.shape[2]
     terms = norm_in[0].astype(F32)
     for z in range(outer):
         for q in range(inner):
@@ -359,7 +366,8 @@
         return dot_tn(lhs, jnp.concatenate([dirs_high, dirs_low, dirs_high], axis=0)) / replicas
 
     def finish(m, lhs, z, block):
-        new_error[0, m, :, columns(z)] = (inputs[m, :, columns(z)] - approx_of(lhs, block)).astype(BF16)
+        error_out[m, :, columns(z)] = (inputs[m, :, columns(z)] - approx_of(lhs, block)).astype(BF16)
+        store(error_out.at[m, :, columns(z)], new_error.at[0, m, :, columns(z)])
 
     dirs_waits = []
     own_side = left_side(basis_own[core])
@@ -370,25 +378,25 @@
         finish(core, own_side, z, block)
 
     right_sum(1, basis, use_own)
-    small[2].wait()
-    small[3].wait()
-    new_weight[core] = weight_in[core] - step_size * approx_of(own_side, dirs_all[1, far, near])
+    own_approx[core] = approx_of(own_side, dirs_all[1, far, near])
     total = norm_part[far]
     for d in range(1, outer):
         norm_far_waits[d - 1].wait_recv()
         total = total + norm_far[d - 1]
     for m in range(2):
-        new_gains[m] = gains_in[m] - step_size * (total[m : m + 1] / replicas)
+        mean_norm[m] = total[m : m + 1] / replicas
     basis_swap.wait_recv()
     other_side = left_side(basis_other[...])
     for dz in range(outer):
         z = far_at(-dz)
         dirs_waits[dz].wait_recv()
         finish(other, other_side, z, jnp.concatenate([dirs_other[z, q] for q in range(inner)], axis=1))
-    new_weight[other] = weight_in[other] - step_size * approx_of(other_side, dirs_other[far, near])
+    own_approx[other] = approx_of(other_side, dirs_other[far, near])
 
     for copy in sends:
         copy.wait_send()
+    for copy in stores:
+        copy.wait()
 
 
 def levels(replicas):
@@ -404,11 +412,12 @@
     chunks = 2
     hbm, vmem = pl.BlockSpec(memory_space=pltpu.HBM), pl.BlockSpec(memory_space=pltpu.VMEM)
     whole = (matrices, rows, width)
-    block = rank // inner
     dma = pltpu.SemaphoreType.DMA
-    factor_copies = 2 * (inner - 1) + outer - 1
+    replicas = outer * inner
+    factor_copies = 2 * (replicas - 1)
+    tile = (SUBLANES, LANES)
     dirs_copies = 2 * outer * (inner - 1) + 2 * (outer - 1)
-    return pl.pallas_call(
+    own_approx, new_error_kv, new_moment_kv, mean_norm = pl.pallas_call(
         functools.partial(kernel, outer, inner, chunks),
         out_shape=(
             jax.ShapeDtypeStruct(weight_kv.shape, F32),
@@ -416,33 +425,36 @@
             jax.ShapeDtypeStruct(moment_kv.shape, BF16),
             jax.ShapeDtypeStruct(norm_gains.shape, F32),
         ),
-        in_specs=[hbm] * 7,
-        out_specs=(vmem,) * 4,
+        in_specs=[hbm] * 5,
+        out_specs=(vmem, hbm, hbm, vmem),
         scratch_shapes=[
             pltpu.VMEM(whole, BF16), pltpu.VMEM(whole, BF16), pltpu.VMEM(whole, BF16),
-            pltpu.VMEM(start_dirs.shape, F32), pltpu.VMEM(weight_kv.shape, F32),
-            pltpu.VMEM(norm_grads.shape, BF16), pltpu.VMEM(norm_gains.shape, F32),
+            pltpu.VMEM(start_dirs.shape, F32), pltpu.VMEM(norm_grads.shape, BF16),
+            pltpu.VMEM(whole, BF16), pltpu.VMEM(whole, BF16),
             pltpu.VMEM(whole, F32), pltpu.VMEM((rows, width), F32),
             pltpu.VMEM(whole, BF16), pltpu.VMEM(whole, BF16),
             pltpu.VMEM((inner, outer, matrices, gain_cols), F32), pltpu.VMEM((inner - 1, outer, matrices, gain_cols), F32),
             pltpu.VMEM((outer, matrices, gain_cols), F32), pltpu.VMEM((outer - 1, matrices, gain_cols), F32),
             pltpu.VMEM((rank, rows), F32), pltpu.VMEM((rank, rows), F32),
-            pltpu.VMEM((2, inner, block, 2 * rows), F32), pltpu.VMEM((2, inner - 1, block, 2 * rows), F32),
-            pltpu.VMEM((2, outer, block, 2 * rows), F32), pltpu.VMEM((2, inner, block, 2 * rows), F32),
+            pltpu.VMEM((2, replicas) + tile, F32), pltpu.VMEM((2, replicas - 1) + tile, F32),
+            pltpu.VMEM((2, replicas) + tile, F32),
             pltpu.VMEM((2, outer, inner, rank, LANES), F32), pltpu.VMEM((2, outer, inner - 1, rank, LANES), F32),
             pltpu.VMEM((2, outer, rank, LANES), F32), pltpu.VMEM((2, outer - 1, rank, LANES), F32),
             pltpu.VMEM((2, outer, inner, rank, LANES), F32),
             pltpu.VMEM((2, rank, rows), F32), pltpu.VMEM((rank, rows), F32),
             pltpu.VMEM((outer, inner, rank, LANES), F32),
-            dma((6 * chunks + 4,)), dma((3 + outer,)), dma((3 + outer,)),
+            dma((6 * chunks + 2,)), dma((2 + 2 * outer,)), dma((3 + outer,)), dma((3 + outer,)),
             dma((inner + outer - 2,)), dma((inner + outer - 2,)),
             dma((2, factor_copies)), dma((2, factor_copies)), dma((2, dirs_copies)), dma((2, dirs_copies)),
         ],
         compiler_params=pltpu.CompilerParams(
-            collective_id=0, has_side_effects=True, vmem_limit_bytes=44 * 2**20
+            collective_id=0, has_side_effects=True, vmem_limit_bytes=62 * 2**20
         ),
         name="power_step",
-    )(grad_kv, error_kv, moment_kv, start_dirs, weight_kv, norm_grads, norm_gains)
+    )(grad_kv, error_kv, moment_kv, start_dirs, norm_grads)
+    new_weight_kv = weight_kv - step_size * own_approx
+    new_gains = norm_gains - step_size * mean_norm
+    return (new_weight_kv, new_error_kv, new_moment_kv, new_gains)
 
 
 def solution(mesh):
@@ -456,7 +468,8 @@
             tensor == matrices == 2
             and near > 1
             and width == LANES * replicas
-            and rank % (SUBLANES * near) == 0
+            and (rank // SUBLANES) * (2 * rows // LANES) == replicas
+            and rank % SUBLANES == 0
             and rows % (2 * LANES) == 0
         )
         return (kernel_shards if fits else plain_shards)(*args)

time: 82.6 us -> 82 us (level)
  local copies, waits for them, and re-layouts: 10.4 us -> 4.64 us
  other arithmetic: 0 us -> 2.91 us
  Pallas kernels: 71.2 us -> 73.6 us
    unnamed x16 -> x8, local copies, waits for them, and re-layouts: 10.4 us -> 4.64 us
    sub x0 -> x2, other arithmetic: none -> 2.91 us  [the longest x1 1.68 us: kernel_shards(): new_weight_kv = weight_kv - step_size * own_approx]
    pallas_call x1, Pallas kernels: 71.2 us -> 73.6 us  [kernel_shards(): pl.pallas_call(functools.partial(kernel, outer, inner, chunks), out_shape...]
where the time goes in v3:
time: 82 us; the launch traced here: 81.8 us
  Pallas kernels  73.6 us (90%)
  local copies, waits for them, and re-layouts  4.64 us (6%)
  other arithmetic  2.91 us (4%)
    pallas_call x1, Pallas kernels, kernel_shards(): pl.pallas_call(functools.partial(kernel, outer, inner, chunks), out_shape...  73.6 us
    unnamed x8, local copies, waits for them, and re-layouts  4.64 us
    sub x1, other arithmetic, kernel_shards(): new_weight_kv = weight_kv - step_size * own_approx  1.68 us

profile of v3, /device:TPU:0, one launch (start us, length us, event | category | flops | bytes accessed | tf_op | source)
XLA Modules:
  0.0 81.8 jit_solution(15956830589527536805)
XLA Ops:
  0.6 0.0 copy-start.2
  0.6 0.0 copy-start.1
  0.7 73.6 %power_step.1 = (f32[2,256,128]{2,1,0:T(8,128)}, bf16[1,2,256,2048]{3,2,1,0:T(8,128)(2,1)}, bf16[1,2,256,2048]{3,2,1,0:T(8,128)(2,1)}, f32[2,1,64]{2,1,0:T(1,128)}) custom-call(bf16[1,2,256,2048]{3,2,1,0:T(8,128)(2,1)} %grad.1, bf16[1,2,256,2048]{3,2,1,0:T(8,128)(2,1)} %error.1, bf16[1,2,256,2048]{3,2,1,0:T(8,128)(2,1)} %moment.1, ...), custom_call_target="tpu_custom_call" | custom-call | tf_op jit(solution)/shard_map/power_step/pallas_call | solution.py:420
  74.3 0.0 copy-done.1
  74.3 1.7 %multiply_subtract_fusion = f32[2,256,128]{2,1,0:T(8,128)} fusion(f32[2,256,128]{2,1,0:T(8,128)S(1)} %copy-done.1, f32[2,256,128]{2,1,0:T(8,128)} %get-tuple-element.8), kind=kLoop, calls=%fused_computation | loop fusion | flops 131072 | bytes 786432 | tf_op jit(solution)/shard_map/sub | solution.py:455
  76.0 0.0 copy-done.2
  76.0 1.2 %multiply_subtract_fusion.1 = f32[2,1,64]{2,1,0:T(1,128)} fusion(f32[2,1,64]{2,1,0:T(1,128)S(1)} %copy-done.2, f32[2,1,64]{2,1,0:T(1,128)} %get-tuple-element.11), kind=kLoop, calls=%fused_computation.1 | loop fusion | flops 256 | bytes 1536 | tf_op jit(solution)/shard_map/sub | solution.py:456
  77.2 0.0 copy-start
  77.2 3.3 %copy.13 = bf16[1,2,256,2048]{3,2,1,0:T(8,128)(2,1)} copy(bf16[1,2,256,2048]{3,2,1,0:T(8,128)(2,1)} %get-tuple-element.17) | data formatting | bytes 4194304
  80.5 0.0 copy-done
  80.5 1.3 %copy.14 = bf16[1,2,256,2048]{3,2,1,0:T(8,128)(2,1)} copy(bf16[1,2,256,2048]{3,2,1,0:T(8,128)(2,1)S(1)} %copy-done) | data formatting | bytes 4194304
Async XLA Ops:
  0.6 75.3 %copy-start.2 = (f32[2,1,64]{2,1,0:T(1,128)S(1)}, f32[2,1,64]{2,1,0:T(1,128)}, u32[]{:S(2)}) copy-start(f32[2,1,64]{2,1,0:T(1,128)} %param.13) | copy-start | bytes 1540
  0.6 73.6 %copy-start.1 = (f32[2,256,128]{2,1,0:T(8,128)S(1)}, f32[2,256,128]{2,1,0:T(8,128)}, u32[]{:S(2)}) copy-start(f32[2,256,128]{2,1,0:T(8,128)} %param.11) | copy-start | bytes 786436
  77.2 3.3 %copy-start = (bf16[1,2,256,2048]{3,2,1,0:T(8,128)(2,1)S(1)}, bf16[1,2,256,2048]{3,2,1,0:T(8,128)(2,1)}, u32[]{:S(2)}) copy-start(bf16[1,2,256,2048]{3,2,1,0:T(8,128)(2,1)} %get-tuple-element.18) | copy-start | bytes 6291460

commit v4 on v3

--- a/solution.py
+++ b/solution.py
@@ -72,32 +72,32 @@
     return lax.dot_general(a, b, (((1,), (1,)), ((), ())), preferred_element_type=F32)
 
 
-def dot_tn(a, b):
-    return lax.dot_general(a, b, (((0,), (0,)), ((), ())), preferred_element_type=F32)
-
-
-def basis_of(factor, block=8):
+def basis_of(factor, table, block=4):
     rank = factor.shape[0]
     gram = lax.dot_general(
         factor, factor, (((1,), (1,)), ((), ())), precision=HIGHEST, preferred_element_type=F32
     )
-    row_id = lax.broadcasted_iota(jnp.int32, (rank, 2 * rank), 0)
-    col_id = lax.broadcasted_iota(jnp.int32, (rank, 2 * rank), 1)
-    unit = (lax.broadcasted_iota(jnp.int32, (rank, rank), 0) == lax.broadcasted_iota(jnp.int32, (rank, rank), 1)).astype(F32)
-    work = jnp.concatenate([gram, unit], axis=1)
+    shape = (SUBLANES, LANES)
+    lane = lax.broadcasted_iota(jnp.int32, (rank, LANES), 1)
+    line = lax.broadcasted_iota(jnp.int32, (rank, LANES), 0)
+    table[...] = jnp.concatenate([gram, (lane == line + rank).astype(F32)[:, rank:]], axis=1)
+    rows = [jnp.broadcast_to(table[i : i + 1, :], shape) for i in range(rank)]
     for first in range(0, rank, block):
-        cols = [jnp.broadcast_to(work[:, j : j + 1], work.shape) for j in range(first, first + block)]
-        rows = [work[j : j + 1, :] for j in range(first, first + block)]
-        for i in range(block):
-            j = first + i
-            ratio = jnp.where(row_id > j, cols[i] * (1.0 / cols[i][j : j + 1, :]), 0.0)
-            for k in range(i + 1, block):
-                cols[k] = cols[k] - ratio * cols[k][j : j + 1, :]
-                rows[k] = rows[k] - ratio[first + k : first + k + 1, :] * rows[i]
-            work = work - ratio * rows[i]
-    pivots = jnp.sum(jnp.where(row_id == col_id, work, 0.0), axis=1, keepdims=True)
-    inverse = work[:, rank:] * lax.rsqrt(pivots)
-    return jnp.dot(inverse, factor, precision=HIGHEST, preferred_element_type=F32)
+        cols = [
+            {i: jnp.broadcast_to(rows[i][:, j : j + 1], shape) for i in range(first, rank)}
+            for j in range(first, first + block)
+        ]
+        for n in range(block):
+            j = first + n
+            pivot = cols[n][j]
+            inverse = 1.0 / pivot
+            for i in range(j + 1, rank):
+                ratio = cols[n][i] * inverse
+                for k in range(n + 1, block):
+                    cols[k][i] = cols[k][i] - ratio * cols[k][j]
+                rows[i] = rows[i] - ratio * rows[j]
+            table[j : j + 1, :] = (rows[j] * lax.rsqrt(pivot))[:1]
+    return jnp.dot(table[:, rank : 2 * rank], factor, precision=HIGHEST, preferred_element_type=F32)
 
 
 def kernel(
@@ -107,7 +107,7 @@
     grad_in, error_in, moment_in, dirs_in, norm_in, moment_out, error_out, inputs, swapped, high, low,
     norm_send, norm_recv, norm_part, norm_far,
     first_send, first_recv, factor_send, factor_recv, factor_all,
-    dirs_send, dirs_near, dirs_part, dirs_far, dirs_all, basis_own, basis_other, dirs_other,
+    dirs_send, dirs_near, dirs_part, dirs_far, dirs_all, basis_own, basis_other, dirs_other, table,
     load_sem, store_sem, swap_ssem, swap_rsem, norm_ssem, norm_rsem, factor_ssem, factor_rsem, dirs_ssem, dirs_rsem,
 ):
     me, core = lax.axis_index("dp"), lax.axis_index("tensor")
@@ -198,8 +198,12 @@
 
     def left_of(dirs, h, cols=slice(None)):
         dirs_high, dirs_low = split(dirs)
-        part = dot_nt(jnp.concatenate([dirs_high, dirs_low], axis=0), high[h, :, cols])
-        return part[:rank] + part[rank:] + dot_nt(dirs_high, low[h, :, cols])
+        both = jnp.concatenate([dirs_high, dirs_low], axis=0)
+        return dot_nt(high[h, :, cols], both), dot_nt(low[h, :, cols], dirs_high)
+
+    def joined(wide, narrow):
+        turned = wide.T
+        return turned[:rank] + turned[rank:] + narrow.T
 
     def left_sum(step, factor, between=None):
         own, arrived, full = factor_send.at[step], factor_recv.at[step], factor_all.at[step]
@@ -300,12 +304,12 @@
 
     form(0, other)
     small[0].wait()
-    first_send[...] = left_of(dirs_in[other], other)
+    first_send[...] = joined(*left_of(dirs_in[other], other))
     pl.semaphore_wait(barrier, len(greeted))
     first_swap = send(first_send, first_recv, swap_ssem.at[0], swap_rsem.at[0], (me, other))
     matrix_swap = send(inputs.at[other], swapped, swap_ssem.at[1], swap_rsem.at[1], (me, other))
     form(1, core)
-    own_left = left_of(dirs_in[core], core)
+    own_left = joined(*left_of(dirs_in[core], core))
 
     small[1].wait()
     gain_cols = mean_norm.shape[2]
@@ -333,13 +337,14 @@
             r = pl.ds(pl.multiple_of(g * 16, 16), 16)
             high[other, r, :], low[other, r, :] = split(swapped[r, :])
 
-    basis = basis_of(left_sum(0, factor, while_summing))
-
-    halves = [jnp.zeros((rank, rows), F32), jnp.zeros((rank, rows), F32)]
+    basis = basis_of(left_sum(0, factor, while_summing), table)
+
+    halves = [(0.0, 0.0), (0.0, 0.0)]
 
     def add_left(dz, z, block):
         for h in range(2):
-            halves[h] = halves[h] + left_of(block, h, columns(z))
+            wide, narrow = left_of(block, h, columns(z))
+            halves[h] = (halves[h][0] + wide, halves[h][1] + narrow)
 
     right_sum(0, basis, add_left)
 
@@ -353,17 +358,18 @@
             k = inner - 1 + d - 1
             norm_far_waits.append(send(norm_part.at[far_at(d)], norm_far.at[d - 1], norm_ssem.at[k], norm_rsem.at[k], far_peer(d)))
 
-    basis = basis_of(left_sum(1, jnp.concatenate(halves, axis=1), norm_step))
+    basis = basis_of(left_sum(1, jnp.concatenate([joined(*half) for half in halves], axis=1), norm_step), table)
     basis_own[0], basis_own[1] = basis[:, :rows], basis[:, rows:]
     basis_swap = send(basis_own.at[other], basis_other, swap_ssem.at[2], swap_rsem.at[2], (me, other))
 
     def left_side(half):
         basis_high, basis_low = split(half)
-        return jnp.concatenate([basis_high, basis_high, basis_low], axis=0)
+        return jnp.concatenate([basis_high, basis_high, basis_low], axis=0).astype(F32).T.astype(BF16)
 
     def approx_of(lhs, block):
         dirs_high, dirs_low = split(block)
-        return dot_tn(lhs, jnp.concatenate([dirs_high, dirs_low, dirs_high], axis=0)) / replicas
+        rhs = jnp.concatenate([dirs_high, dirs_low, dirs_high], axis=0)
+        return jnp.dot(lhs, rhs, preferred_element_type=F32) / replicas
 
     def finish(m, lhs, z, block):
         error_out[m, :, columns(z)] = (inputs[m, :, columns(z)] - approx_of(lhs, block)).astype(BF16)
@@ -442,13 +448,13 @@
             pltpu.VMEM((2, outer, rank, LANES), F32), pltpu.VMEM((2, outer - 1, rank, LANES), F32),
             pltpu.VMEM((2, outer, inner, rank, LANES), F32),
             pltpu.VMEM((2, rank, rows), F32), pltpu.VMEM((rank, rows), F32),
-            pltpu.VMEM((outer, inner, rank, LANES), F32),
+            pltpu.VMEM((outer, inner, rank, LANES), F32), pltpu.VMEM((rank, LANES), F32),
             dma((6 * chunks + 2,)), dma((2 + 2 * outer,)), dma((3 + outer,)), dma((3 + outer,)),
             dma((inner + outer - 2,)), dma((inner + outer - 2,)),
             dma((2, factor_copies)), dma((2, factor_copies)), dma((2, dirs_copies)), dma((2, dirs_copies)),
         ],
         compiler_params=pltpu.CompilerParams(
-            collective_id=0, has_side_effects=True, vmem_limit_bytes=62 * 2**20
+            collective_id=0, has_side_effects=True, vmem_limit_bytes=48 * 2**20
         ),
         name="power_step",
     )(grad_kv, error_kv, moment_kv, start_dirs, norm_grads)

time: 82 us -> 80.2 us (0.978)
  other arithmetic: 2.91 us -> 1.31 us
    sub x1, other arithmetic: 1.68 us -> 0.75 us  [kernel_shards(): new_weight_kv = weight_kv - step_size * own_approx]
    unnamed x8 -> x10, local copies, waits for them, and re-layouts: 4.64 us -> 4.37 us
where the time goes in v4:
time: 80.2 us; the launch traced here: 80.1 us
  Pallas kernels  73.7 us (92%)
  local copies, waits for them, and re-layouts  4.37 us (5%)
  other arithmetic  1.31 us (2%)
    pallas_call x1, Pallas kernels, kernel_shards(): pl.pallas_call(functools.partial(kernel, outer, inner, chunks), out_shape...  73.7 us
    unnamed x10, local copies, waits for them, and re-layouts  4.37 us

profile of v4, /device:TPU:0, one launch (start us, length us, event | category | flops | bytes accessed | tf_op | source)
XLA Modules:
  0.0 80.1 jit_solution(1662757077197321159)
XLA Ops:
  0.6 0.0 copy-start
  0.6 1.0 %copy-done = f32[2,32,2048]{2,1,0:T(8,128)S(1)} copy-done((f32[2,32,2048]{2,1,0:T(8,128)S(1)}, f32[2,32,2048]{2,1,0:T(8,128)}, u32[]{:S(2)}) %copy-start) | copy-done | bytes 524312
  1.7 0.0 copy-start.1
  1.7 0.7 copy-done.1
  2.4 0.0 copy-start.2
  2.4 0.0 copy-start.3
  2.4 73.7 %power_step.1 = (f32[2,256,128]{2,1,0:T(8,128)S(1)}, bf16[1,2,256,2048]{3,2,1,0:T(8,128)(2,1)S(1)}, bf16[1,2,256,2048]{3,2,1,0:T(8,128)(2,1)S(1)}, f32[2,1,64]{2,1,0:T(1,128)S(1)}) custom-call(bf16[1,2,256,2048]{3,2,1,0:T(8,128)(2,1)} %grad.1, bf16[1,2,256,2048]{3,2,1,0:T(8,128)(2,1)} %error.1, bf16[1,2,256,2048]{3,2,1,0:T(8,128)(2,1)} %moment.1, ...), custom_call_target="tpu_custom_call" | custom-call | tf_op jit(solution)/shard_map/power_step/pallas_call | solution.py:426
  76.1 0.0 copy-done.2
  76.1 0.7 multiply_subtract_fusion
  76.8 0.0 copy-done.3
  76.8 0.6 multiply_subtract_fusion.1
  77.4 1.3 %copy.13 = bf16[1,2,256,2048]{3,2,1,0:T(8,128)(2,1)} copy(bf16[1,2,256,2048]{3,2,1,0:T(8,128)(2,1)S(1)} %get-tuple-element.17) | data formatting | bytes 4194304
  78.7 1.3 %copy.14 = bf16[1,2,256,2048]{3,2,1,0:T(8,128)(2,1)} copy(bf16[1,2,256,2048]{3,2,1,0:T(8,128)(2,1)S(1)} %get-tuple-element.18) | data formatting | bytes 4194304
Async XLA Ops:
  0.6 1.0 %copy-start = (f32[2,32,2048]{2,1,0:T(8,128)S(1)}, f32[2,32,2048]{2,1,0:T(8,128)}, u32[]{:S(2)}) copy-start(f32[2,32,2048]{2,1,0:T(8,128)} %start_dirs.1) | copy-start | bytes 1572868
  1.7 0.7 copy-start.1
  2.4 73.7 %copy-start.2 = (f32[2,256,128]{2,1,0:T(8,128)S(1)}, f32[2,256,128]{2,1,0:T(8,128)}, u32[]{:S(2)}) copy-start(f32[2,256,128]{2,1,0:T(8,128)} %param.11) | copy-start | bytes 786436
  2.4 74.5 %copy-start.3 = (f32[2,1,64]{2,1,0:T(1,128)S(1)}, f32[2,1,64]{2,1,0:T(1,128)}, u32[]{:S(2)}) copy-start(f32[2,1,64]{2,1,0:T(1,128)} %param.13) | copy-start | bytes 1540

commit v5 on v4

--- a/solution.py
+++ b/solution.py
@@ -107,7 +107,7 @@
     grad_in, error_in, moment_in, dirs_in, norm_in, moment_out, error_out, inputs, swapped, high, low,
     norm_send, norm_recv, norm_part, norm_far,
     first_send, first_recv, factor_send, factor_recv, factor_all,
-    dirs_send, dirs_near, dirs_part, dirs_far, dirs_all, basis_own, basis_other, dirs_other, table,
+    dirs_send, dirs_recv, dirs_all, basis_own, basis_other, dirs_other, table,
     load_sem, store_sem, swap_ssem, swap_rsem, norm_ssem, norm_rsem, factor_ssem, factor_rsem, dirs_ssem, dirs_rsem,
 ):
     me, core = lax.axis_index("dp"), lax.axis_index("tensor")
@@ -239,13 +239,15 @@
     def right_sum(step, basis, consume):
         basis_high, basis_low = split(basis)
         both = jnp.concatenate([basis_high, basis_low], axis=0)
-        own, arrived, part, other_far, full = (
-            dirs_send.at[step], dirs_near.at[step], dirs_part.at[step], dirs_far.at[step], dirs_all.at[step]
-        )
+        own, arrived, full = dirs_send.at[step], dirs_recv.at[step], dirs_all.at[step]
         ssem, rsem = dirs_ssem.at[step], dirs_rsem.at[step]
-        order = list(range(1, outer)) + [0]
-        waits = {}
-        for dz in order:
+        steps = [(dz, dq) for dz in list(range(1, outer)) + [0] for dq in range(inner) if dz or dq]
+        waits = []
+
+        def place(dz, dq):
+            return (far_at(dz) * inner + near_at(dq), core)
+
+        for dz in list(range(1, outer)) + [0]:
             z = far_at(dz)
             sums = low_sums = 0.0
             for h in range(2):
@@ -255,59 +257,34 @@
             block = sums[:rank] + sums[rank:] + low_sums
             for q in range(inner):
                 own[z, q] = block[:, q * LANES : (q + 1) * LANES]
-            for d in range(1, inner):
-                k = dz * (inner - 1) + d - 1
-                waits[dz, d] = send(own.at[z, near_at(d)], arrived.at[z, d - 1], ssem.at[k], rsem.at[k], near_peer(d))
-        base = outer * (inner - 1)
-        far_waits = []
-        for dz in order:
-            z = far_at(dz)
-            total = own[z, near]
-            for d in range(1, inner):
-                waits[dz, d].wait_recv()
-                total = total + arrived[z, d - 1]
-            if dz:
-                part[z] = total
-                k = base + dz - 1
-                far_waits.append(send(part.at[z], other_far.at[dz - 1], ssem.at[k], rsem.at[k], far_peer(dz)))
-        for dz in range(1, outer):
-            far_waits[dz - 1].wait_recv()
-            total = total + other_far[dz - 1]
+            for dq in range(inner):
+                if dz or dq:
+                    k = dz * inner + dq - 1
+                    waits.append(send(own.at[z, near_at(dq)], arrived.at[k], ssem.at[k], rsem.at[k], place(dz, dq)))
+        for copy in waits:
+            copy.wait_recv()
+        total = own[far, near]
+        for k in range(replicas - 1):
+            total = total + arrived[k]
         full[far, near] = total
-        base += outer - 1
-        for dz in range(1, outer):
-            k = base + dz - 1
-            send(full.at[far, near], full.at[far, near], ssem.at[k], rsem.at[k], far_peer(dz))
-        spread = base + outer - 1
-
-        def forward(dz):
-            for d in range(1, inner):
-                k = spread + dz * (inner - 1) + d - 1
-                slot = full.at[far_at(-dz), near]
-                send(slot, slot, ssem.at[k], rsem.at[k], near_peer(d))
-
-        def take(dz):
+        base = replicas - 1
+        for dz, dq in steps:
+            k = base + dz * inner + dq - 1
+            send(full.at[far, near], full.at[far, near], ssem.at[k], rsem.at[k], place(dz, dq))
+        for dz in range(outer):
             z = far_at(-dz)
-            for d in range(1, inner):
-                k = spread + dz * (inner - 1) + d - 1
-                slot = full.at[z, near_at(-d)]
-                remote(slot, slot, ssem.at[k], rsem.at[k], near_peer(d)).wait_recv()
+            for dq in range(inner):
+                if dz or dq:
+                    k = base + dz * inner + dq - 1
+                    slot = full.at[z, near_at(-dq)]
+                    remote(slot, slot, ssem.at[k], rsem.at[k], place(dz, dq)).wait_recv()
             consume(dz, z, jnp.concatenate([full[z, q] for q in range(inner)], axis=1))
-
-        forward(0)
-        for dz in range(1, outer):
-            slot = full.at[far_at(-dz), near]
-            remote(slot, slot, ssem.at[base + dz - 1], rsem.at[base + dz - 1], far_peer(dz)).wait_recv()
-            forward(dz)
-            take(dz - 1)
-        take(outer - 1)
 
     form(0, other)
     small[0].wait()
     first_send[...] = joined(*left_of(dirs_in[other], other))
     pl.semaphore_wait(barrier, len(greeted))
     first_swap = send(first_send, first_recv, swap_ssem.at[0], swap_rsem.at[0], (me, other))
-    matrix_swap = send(inputs.at[other], swapped, swap_ssem.at[1], swap_rsem.at[1], (me, other))
     form(1, core)
     own_left = joined(*left_of(dirs_in[core], core))
 
@@ -325,19 +302,20 @@
         jnp.where(core == 0, own_left, their_left), jnp.where(core == 0, their_left, own_left)
     ], axis=1)
 
-    norm_waits, norm_far_waits = [], []
+    norm_waits, norm_far_waits, matrix_swap = [], [], []
 
     def while_summing():
         for d in range(1, inner):
             norm_waits.append(send(norm_send.at[near_at(d)], norm_recv.at[d - 1], norm_ssem.at[d - 1], norm_rsem.at[d - 1], near_peer(d)))
-        matrix_swap.wait_recv()
-
-        @pl.loop(0, rows // 16)
-        def _(g):
-            r = pl.ds(pl.multiple_of(g * 16, 16), 16)
-            high[other, r, :], low[other, r, :] = split(swapped[r, :])
+        matrix_swap.append(send(inputs.at[other], swapped, swap_ssem.at[1], swap_rsem.at[1], (me, other)))
 
     basis = basis_of(left_sum(0, factor, while_summing), table)
+    matrix_swap[0].wait_recv()
+
+    @pl.loop(0, rows // 16)
+    def _(g):
+        r = pl.ds(pl.multiple_of(g * 16, 16), 16)
+        high[other, r, :], low[other, r, :] = split(swapped[r, :])
 
     halves = [(0.0, 0.0), (0.0, 0.0)]
 
@@ -420,9 +398,8 @@
     whole = (matrices, rows, width)
     dma = pltpu.SemaphoreType.DMA
     replicas = outer * inner
-    factor_copies = 2 * (replicas - 1)
+    sum_copies = 2 * (replicas - 1)
     tile = (SUBLANES, LANES)
-    dirs_copies = 2 * outer * (inner - 1) + 2 * (outer - 1)
     own_approx, new_error_kv, new_moment_kv, mean_norm = pl.pallas_call(
         functools.partial(kernel, outer, inner, chunks),
         out_shape=(
@@ -444,14 +421,13 @@
             pltpu.VMEM((rank, rows), F32), pltpu.VMEM((rank, rows), F32),
             pltpu.VMEM((2, replicas) + tile, F32), pltpu.VMEM((2, replicas - 1) + tile, F32),
             pltpu.VMEM((2, replicas) + tile, F32),
-            pltpu.VMEM((2, outer, inner, rank, LANES), F32), pltpu.VMEM((2, outer, inner - 1, rank, LANES), F32),
-            pltpu.VMEM((2, outer, rank, LANES), F32), pltpu.VMEM((2, outer - 1, rank, LANES), F32),
+            pltpu.VMEM((2, outer, inner, rank, LANES), F32), pltpu.VMEM((2, replicas - 1, rank, LANES), F32),
             pltpu.VMEM((2, outer, inner, rank, LANES), F32),
             pltpu.VMEM((2, rank, rows), F32), pltpu.VMEM((rank, rows), F32),
             pltpu.VMEM((outer, inner, rank, LANES), F32), pltpu.VMEM((rank, LANES), F32),
             dma((6 * chunks + 2,)), dma((2 + 2 * outer,)), dma((3 + outer,)), dma((3 + outer,)),
             dma((inner + outer - 2,)), dma((inner + outer - 2,)),
-            dma((2, factor_copies)), dma((2, factor_copies)), dma((2, dirs_copies)), dma((2, dirs_copies)),
+            dma((2, sum_copies)), dma((2, sum_copies)), dma((2, sum_copies)), dma((2, sum_copies)),
         ],
         compiler_params=pltpu.CompilerParams(
             collective_id=0, has_side_effects=True, vmem_limit_bytes=48 * 2**20

time: 80.2 us -> 71 us (0.89)
  Pallas kernels: 73.7 us -> 64.5 us
    pallas_call x1, Pallas kernels: 73.7 us -> 64.5 us  [kernel_shards(): pl.pallas_call(functools.partial(kernel, outer, inner, chunks), out_shape...]
where the time goes in v5:
time: 71 us; the launch traced here: 70.8 us
  Pallas kernels  64.5 us (91%)
  local copies, waits for them, and re-layouts  4.37 us (6%)
  other arithmetic  1.31 us (2%)
    pallas_call x1, Pallas kernels, kernel_shards(): pl.pallas_call(functools.partial(kernel, outer, inner, chunks), out_shape...  64.5 us
    unnamed x10, local copies, waits for them, and re-layouts  4.37 us

profile of v5, /device:TPU:0, one launch (start us, length us, event | category | flops | bytes accessed | tf_op | source)
XLA Modules:
  0.0 70.8 jit_solution(13952827463443366211)
XLA Ops:
  0.6 0.0 copy-start
  0.6 1.0 %copy-done = f32[2,32,2048]{2,1,0:T(8,128)S(1)} copy-done((f32[2,32,2048]{2,1,0:T(8,128)S(1)}, f32[2,32,2048]{2,1,0:T(8,128)}, u32[]{:S(2)}) %copy-start) | copy-done | bytes 524312
  1.7 0.0 copy-start.1
  1.7 0.7 copy-done.1
  2.4 0.0 copy-start.2
  2.4 0.0 copy-start.3
  2.4 64.5 %power_step.1 = (f32[2,256,128]{2,1,0:T(8,128)S(1)}, bf16[1,2,256,2048]{3,2,1,0:T(8,128)(2,1)S(1)}, bf16[1,2,256,2048]{3,2,1,0:T(8,128)(2,1)S(1)}, f32[2,1,64]{2,1,0:T(1,128)S(1)}) custom-call(bf16[1,2,256,2048]{3,2,1,0:T(8,128)(2,1)} %grad.1, bf16[1,2,256,2048]{3,2,1,0:T(8,128)(2,1)} %error.1, bf16[1,2,256,2048]{3,2,1,0:T(8,128)(2,1)} %moment.1, ...), custom_call_target="tpu_custom_call" | custom-call | tf_op jit(solution)/shard_map/power_step/pallas_call | solution.py:403
  66.9 0.0 copy-done.2
  66.9 0.7 %multiply_subtract_fusion = f32[2,256,128]{2,1,0:T(8,128)} fusion(f32[2,256,128]{2,1,0:T(8,128)S(1)} %copy-done.2, f32[2,256,128]{2,1,0:T(8,128)S(1)} %get-tuple-element.8), kind=kLoop, calls=%fused_computation | loop fusion | flops 131072 | bytes 786432 | tf_op jit(solution)/shard_map/sub | solution.py:437
  67.6 0.0 copy-done.3
  67.6 0.6 multiply_subtract_fusion.1
  68.2 1.3 %copy.13 = bf16[1,2,256,2048]{3,2,1,0:T(8,128)(2,1)} copy(bf16[1,2,256,2048]{3,2,1,0:T(8,128)(2,1)S(1)} %get-tuple-element.17) | data formatting | bytes 4194304
  69.5 1.3 %copy.14 = bf16[1,2,256,2048]{3,2,1,0:T(8,128)(2,1)} copy(bf16[1,2,256,2048]{3,2,1,0:T(8,128)(2,1)S(1)} %get-tuple-element.18) | data formatting | bytes 4194304
Async XLA Ops:
  0.6 1.0 %copy-start = (f32[2,32,2048]{2,1,0:T(8,128)S(1)}, f32[2,32,2048]{2,1,0:T(8,128)}, u32[]{:S(2)}) copy-start(f32[2,32,2048]{2,1,0:T(8,128)} %start_dirs.1) | copy-start | bytes 1572868
  1.7 0.7 copy-start.1
  2.4 64.5 %copy-start.2 = (f32[2,256,128]{2,1,0:T(8,128)S(1)}, f32[2,256,128]{2,1,0:T(8,128)}, u32[]{:S(2)}) copy-start(f32[2,256,128]{2,1,0:T(8,128)} %param.11) | copy-start | bytes 786436
  2.4 65.3 %copy-start.3 = (f32[2,1,64]{2,1,0:T(1,128)S(1)}, f32[2,1,64]{2,1,0:T(1,128)}, u32[]{:S(2)}) copy-start(f32[2,1,64]{2,1,0:T(1,128)} %param.13) | copy-start | bytes 1540

commit v6 on v5

--- a/solution.py
+++ b/solution.py
@@ -108,7 +108,7 @@
     norm_send, norm_recv, norm_part, norm_far,
     first_send, first_recv, factor_send, factor_recv, factor_all,
     dirs_send, dirs_recv, dirs_all, basis_own, basis_other, dirs_other, table,
-    load_sem, store_sem, swap_ssem, swap_rsem, norm_ssem, norm_rsem, factor_ssem, factor_rsem, dirs_ssem, dirs_rsem,
+    first_ssem, first_rsem, load_sem, store_sem, swap_ssem, swap_rsem, norm_ssem, norm_rsem, factor_ssem, factor_rsem, dirs_ssem, dirs_rsem,
 ):
     me, core = lax.axis_index("dp"), lax.axis_index("tensor")
     other = 1 - core
@@ -176,7 +176,7 @@
             small[1].start()
 
     barrier = pltpu.get_barrier_semaphore()
-    greeted = [peer(d) for d in range(1, replicas)] + [(me, other)]
+    greeted = [(peer(d)[0], c) for d in range(1, replicas) for c in (core, other)] + [(me, other)]
     for device in greeted:
         pl.semaphore_signal(barrier, inc=1, device_id=device, device_id_type=pl.DeviceIdType.MESH)
 
@@ -205,27 +205,47 @@
         turned = wide.T
         return turned[:rank] + turned[rank:] + narrow.T
 
-    def left_sum(step, factor, between=None):
-        own, arrived, full = factor_send.at[step], factor_recv.at[step], factor_all.at[step]
-        ssem, rsem = factor_ssem.at[step], factor_rsem.at[step]
-        row_blocks = 2 * rows // LANES
-        for j in range(replicas):
-            a, b = divmod(j, row_blocks)
-            own[j] = factor[a * SUBLANES : (a + 1) * SUBLANES, b * LANES : (b + 1) * LANES]
-        order = sorted(range(1, replicas), key=lambda d: abs(2 * d - replicas))
-        waits = [send(own.at[peer(d)[0]], arrived.at[d - 1], ssem.at[d - 1], rsem.at[d - 1], peer(d)) for d in order]
-        if between is not None:
-            between()
-        for copy in waits:
-            copy.wait_recv()
-        total = own[me]
-        for d in range(1, replicas):
-            total = total + arrived[d - 1]
+    row_blocks = 2 * rows // LANES
+    half_blocks = row_blocks // 2
+    far_first = sorted(range(1, replicas), key=lambda d: abs(2 * d - replicas))
+    own_tiles = [(a, b) for a in range(rank // SUBLANES) for b in range(half_blocks)]
+    first_waits = []
+
+    def first_scatter(i, m, factor):
+        for n, (a, b) in enumerate(own_tiles):
+            j = a * row_blocks + core * half_blocks + b
+            k = i * len(own_tiles) + n
+            first_send[k] = factor[a * SUBLANES : (a + 1) * SUBLANES, b * LANES : (b + 1) * LANES]
+            copy = remote(first_send.at[k], first_recv.at[me], first_ssem.at[k], first_rsem.at[me], (j, m))
+            if i == 0:
+                copy.start()
+                sends.append(copy)
+            else:
+                pl.when(j != me)(copy.start)
+                first_waits.append((j, copy))
+
+                @pl.when(j == me)
+                def _():
+                    first_recv[me] = first_send[k]
+
+    def first_sum():
+        here = lax.div(lax.rem(me, row_blocks), half_blocks) == core
+        for n in range(replicas):
+            slot = first_recv.at[n]
+            copy = remote(slot, slot, first_ssem.at[0], first_rsem.at[n], (me, other))
+            pl.when(jnp.logical_not(jnp.logical_and(here, me == n)))(copy.wait_recv)
+        total = first_recv[0]
+        for n in range(1, replicas):
+            total = total + first_recv[n]
+        return left_spread(0, total)
+
+    def left_spread(step, total):
+        full, ssem, rsem = factor_all.at[step], factor_ssem.at[step], factor_rsem.at[step]
         full[me] = total
         base = replicas - 1
-        for d in order:
+        for d in far_first:
             send(full.at[me], full.at[me], ssem.at[base + d - 1], rsem.at[base + d - 1], peer(d))
-        for d in order:
+        for d in far_first:
             slot = full.at[peer(-d)[0]]
             remote(slot, slot, ssem.at[base + d - 1], rsem.at[base + d - 1], peer(d)).wait_recv()
         return jnp.concatenate(
@@ -235,6 +255,21 @@
             ],
             axis=0,
         )
+
+    def left_sum(factor, between):
+        own, arrived = factor_send.at[1], factor_recv.at[1]
+        ssem, rsem = factor_ssem.at[1], factor_rsem.at[1]
+        for j in range(replicas):
+            a, b = divmod(j, row_blocks)
+            own[j] = factor[a * SUBLANES : (a + 1) * SUBLANES, b * LANES : (b + 1) * LANES]
+        waits = [send(own.at[peer(d)[0]], arrived.at[d - 1], ssem.at[d - 1], rsem.at[d - 1], peer(d)) for d in far_first]
+        between()
+        for copy in waits:
+            copy.wait_recv()
+        total = own[me]
+        for d in range(1, replicas):
+            total = total + arrived[d - 1]
+        return left_spread(1, total)
 
     def right_sum(step, basis, consume):
         basis_high, basis_low = split(basis)
@@ -282,11 +317,12 @@
 
     form(0, other)
     small[0].wait()
-    first_send[...] = joined(*left_of(dirs_in[other], other))
+    their_left = joined(*left_of(dirs_in[other], other))
     pl.semaphore_wait(barrier, len(greeted))
-    first_swap = send(first_send, first_recv, swap_ssem.at[0], swap_rsem.at[0], (me, other))
+    first_scatter(0, other, their_left)
     form(1, core)
-    own_left = joined(*left_of(dirs_in[core], core))
+    first_scatter(1, core, joined(*left_of(dirs_in[core], core)))
+    matrix_swap = send(inputs.at[other], swapped, swap_ssem.at[1], swap_rsem.at[1], (me, other))
 
     small[1].wait()
     gain_cols = mean_norm.shape[2]
@@ -296,21 +332,11 @@
             p = z * inner + q
             norm_send[q, z] = terms[:, p * gain_cols : (p + 1) * gain_cols]
 
-    first_swap.wait_recv()
-    their_left = first_recv[...]
-    factor = jnp.concatenate([
-        jnp.where(core == 0, own_left, their_left), jnp.where(core == 0, their_left, own_left)
-    ], axis=1)
-
-    norm_waits, norm_far_waits, matrix_swap = [], [], []
-
-    def while_summing():
-        for d in range(1, inner):
-            norm_waits.append(send(norm_send.at[near_at(d)], norm_recv.at[d - 1], norm_ssem.at[d - 1], norm_rsem.at[d - 1], near_peer(d)))
-        matrix_swap.append(send(inputs.at[other], swapped, swap_ssem.at[1], swap_rsem.at[1], (me, other)))
-
-    basis = basis_of(left_sum(0, factor, while_summing), table)
-    matrix_swap[0].wait_recv()
+    norm_waits, norm_far_waits = [], []
+    for d in range(1, inner):
+        norm_waits.append(send(norm_send.at[near_at(d)], norm_recv.at[d - 1], norm_ssem.at[d - 1], norm_rsem.at[d - 1], near_peer(d)))
+    basis = basis_of(first_sum(), table)
+    matrix_swap.wait_recv()
 
     @pl.loop(0, rows // 16)
     def _(g):
@@ -336,7 +362,7 @@
             k = inner - 1 + d - 1
             norm_far_waits.append(send(norm_part.at[far_at(d)], norm_far.at[d - 1], norm_ssem.at[k], norm_rsem.at[k], far_peer(d)))
 
-    basis = basis_of(left_sum(1, jnp.concatenate([joined(*half) for half in halves], axis=1), norm_step), table)
+    basis = basis_of(left_sum(jnp.concatenate([joined(*half) for half in halves], axis=1), norm_step), table)
     basis_own[0], basis_own[1] = basis[:, :rows], basis[:, rows:]
     basis_swap = send(basis_own.at[other], basis_other, swap_ssem.at[2], swap_rsem.at[2], (me, other))
 
@@ -379,6 +405,8 @@
 
     for copy in sends:
         copy.wait_send()
+    for j, copy in first_waits:
+        pl.when(j != me)(copy.wait_send)
     for copy in stores:
         copy.wait()
 
@@ -418,14 +446,14 @@
             pltpu.VMEM(whole, BF16), pltpu.VMEM(whole, BF16),
             pltpu.VMEM((inner, outer, matrices, gain_cols), F32), pltpu.VMEM((inner - 1, outer, matrices, gain_cols), F32),
             pltpu.VMEM((outer, matrices, gain_cols), F32), pltpu.VMEM((outer - 1, matrices, gain_cols), F32),
-            pltpu.VMEM((rank, rows), F32), pltpu.VMEM((rank, rows), F32),
+            pltpu.VMEM((replicas,) + tile, F32), pltpu.VMEM((replicas,) + tile, F32),
             pltpu.VMEM((2, replicas) + tile, F32), pltpu.VMEM((2, replicas - 1) + tile, F32),
             pltpu.VMEM((2, replicas) + tile, F32),
             pltpu.VMEM((2, outer, inner, rank, LANES), F32), pltpu.VMEM((2, replicas - 1, rank, LANES), F32),
             pltpu.VMEM((2, outer, inner, rank, LANES), F32),
             pltpu.VMEM((2, rank, rows), F32), pltpu.VMEM((rank, rows), F32),
             pltpu.VMEM((outer, inner, rank, LANES), F32), pltpu.VMEM((rank, LANES), F32),
-            dma((6 * chunks + 2,)), dma((2 + 2 * outer,)), dma((3 + outer,)), dma((3 + outer,)),
+            dma((replicas,)), dma((replicas,)), dma((6 * chunks + 2,)), dma((2 + 2 * outer,)), dma((3 + outer,)), dma((3 + outer,)),
             dma((inner + outer - 2,)), dma((inner + outer - 2,)),
             dma((2, sum_copies)), dma((2, sum_copies)), dma((2, sum_copies)), dma((2, sum_copies)),
         ],

time: 71 us -> 70.9 us (level)
  no operation moved by 1% of the time
where the time goes in v6:
time: 70.9 us; the launch traced here: 70.7 us
  Pallas kernels  64.4 us (91%)
  local copies, waits for them, and re-layouts  4.37 us (6%)
  other arithmetic  1.31 us (2%)
    pallas_call x1, Pallas kernels, kernel_shards(): pl.pallas_call(functools.partial(kernel, outer, inner, chunks), out_shape...  64.4 us
    unnamed x10, local copies, waits for them, and re-layouts  4.37 us

profile of v6, /device:TPU:0, one launch (start us, length us, event | category | flops | bytes accessed | tf_op | source)
XLA Modules:
  0.0 70.7 jit_solution(12965186055876231484)
XLA Ops:
  0.6 0.0 copy-start
  0.6 1.0 %copy-done = f32[2,32,2048]{2,1,0:T(8,128)S(1)} copy-done((f32[2,32,2048]{2,1,0:T(8,128)S(1)}, f32[2,32,2048]{2,1,0:T(8,128)}, u32[]{:S(2)}) %copy-start) | copy-done | bytes 524312
  1.7 0.0 copy-start.1
  1.7 0.7 copy-done.1
  2.4 0.0 copy-start.2
  2.4 0.0 copy-start.3
  2.4 64.4 %power_step.1 = (f32[2,256,128]{2,1,0:T(8,128)S(1)}, bf16[1,2,256,2048]{3,2,1,0:T(8,128)(2,1)S(1)}, bf16[1,2,256,2048]{3,2,1,0:T(8,128)(2,1)S(1)}, f32[2,1,64]{2,1,0:T(1,128)S(1)}) custom-call(bf16[1,2,256,2048]{3,2,1,0:T(8,128)(2,1)} %grad.1, bf16[1,2,256,2048]{3,2,1,0:T(8,128)(2,1)} %error.1, bf16[1,2,256,2048]{3,2,1,0:T(8,128)(2,1)} %moment.1, ...), custom_call_target="tpu_custom_call" | custom-call | tf_op jit(solution)/shard_map/power_step/pallas_call | solution.py:431
  66.7 0.0 copy-done.2
  66.8 0.7 %multiply_subtract_fusion = f32[2,256,128]{2,1,0:T(8,128)} fusion(f32[2,256,128]{2,1,0:T(8,128)S(1)} %copy-done.2, f32[2,256,128]{2,1,0:T(8,128)S(1)} %get-tuple-element.8), kind=kLoop, calls=%fused_computation | loop fusion | flops 131072 | bytes 786432 | tf_op jit(solution)/shard_map/sub | solution.py:465
  67.5 0.0 copy-done.3
  67.5 0.6 multiply_subtract_fusion.1
  68.1 1.3 %copy.13 = bf16[1,2,256,2048]{3,2,1,0:T(8,128)(2,1)} copy(bf16[1,2,256,2048]{3,2,1,0:T(8,128)(2,1)S(1)} %get-tuple-element.17) | data formatting | bytes 4194304
  69.4 1.3 %copy.14 = bf16[1,2,256,2048]{3,2,1,0:T(8,128)(2,1)} copy(bf16[1,2,256,2048]{3,2,1,0:T(8,128)(2,1)S(1)} %get-tuple-element.18) | data formatting | bytes 4194304
Async XLA Ops:
  0.6 1.0 %copy-start = (f32[2,32,2048]{2,1,0:T(8,128)S(1)}, f32[2,32,2048]{2,1,0:T(8,128)}, u32[]{:S(2)}) copy-start(f32[2,32,2048]{2,1,0:T(8,128)} %start_dirs.1) | copy-start | bytes 1572868
  1.7 0.7 copy-start.1
  2.4 64.4 %copy-start.2 = (f32[2,256,128]{2,1,0:T(8,128)S(1)}, f32[2,256,128]{2,1,0:T(8,128)}, u32[]{:S(2)}) copy-start(f32[2,256,128]{2,1,0:T(8,128)} %param.11) | copy-start | bytes 786436
  2.4 65.1 %copy-start.3 = (f32[2,1,64]{2,1,0:T(1,128)S(1)}, f32[2,1,64]{2,1,0:T(1,128)}, u32[]{:S(2)}) copy-start(f32[2,1,64]{2,1,0:T(1,128)} %param.13) | copy-start | bytes 1540
